TPU v7x, 256 devices: a whole 4x4x8 slice. The times are simulated.
256 devices in a mesh: seq: 32 (over x, y, core), doc: 8 (over z).
Axes of the slice: x: 4, y: 4, z: 8, core: 2. Of those that a mesh axis runs over, the one named last changes fastest.
Arguments:
- q_self: bfloat16 [8, 4096, 4096], P('doc', 'seq'), may hold values from -6 to 6, as said below
- k_self: bfloat16 [8, 4096, 4096], P('doc', 'seq'), may hold values from -6 to 6, as said below
- v_self: bfloat16 [8, 4096, 4096], P('doc', 'seq'), may hold values from -6 to 6
- q_cross: bfloat16 [8, 4096, 4096], P('doc', 'seq'), may hold values from -6 to 6, as said below
- latents: bfloat16 [8, 32, 2, 64, 4096], P('doc', 'seq'), may hold values from -6 to 6, as said below
- media: int32 [8, 4096], P('doc', 'seq'), may hold values from -1 to 31, as said below
- gate: float32 [4096], replicated, may hold values from -1.2 to 1.2
- cotangent: bfloat16 [8, 4096, 4096], P('doc', 'seq'), may hold values from -6 to 6
Outputs:
- out: bfloat16 [8, 4096, 4096], P('doc', 'seq')
- grad_q_self: bfloat16 [8, 4096, 4096], P('doc', 'seq')
- grad_k_self: bfloat16 [8, 4096, 4096], P('doc', 'seq')
- grad_v_self: bfloat16 [8, 4096, 4096], P('doc', 'seq')
- grad_q_cross: bfloat16 [8, 4096, 4096], P('doc', 'seq')
- grad_latents: bfloat16 [8, 32, 2, 64, 4096], P('doc', 'seq')
- gate_grad: float32 [4096], replicated
Inputs may be any that keep to these rules, and one draw needn't show every extreme that they name: `media`: each document uses its first 1 to 8 slots, placed at distinct positions of the document in slot order, and the last document of each sequence uses all 8; a token holds the slot of the last of them at or before it, or -1 if none, so values never fall within a document and stay inside its own slots. `q_self`: entries are of order one. `k_self`: entries are of order one. `q_cross`: entries are of order one. `latents`: entries are of order one.
All inputs are finite; a program needn't handle non-finite values.
Results may differ from a plain program's by a relative error of at most 0.01.
Values may be sent and summed in bfloat16 or wider, within the bound.
A program may use at most 128 MiB of HBM per device.

v0:
```python
import jax
import jax.numpy as jnp
from jax import lax
from jax.sharding import PartitionSpec as P

E = 128
LAT = 64
MEDIA = 8
DOC_LEN = 1024


NEG_FILL = -1e30


def product(form, left, right):
    return jnp.einsum(form, left, right, preferred_element_type=jnp.float32)


def self_document(inputs):
    query_rows, key_rows, value_rows, grad_rows = inputs
    factor = query_rows.shape[-1] ** (-0.5)
    score_full = factor * product("qhe,khe->hqk", query_rows, key_rows)
    places = jnp.arange(query_rows.shape[0], dtype=jnp.int32)
    causal = places[None, :] <= places[:, None]
    score_full = jnp.where(causal[None], score_full, -jnp.inf)
    weight_full = jnp.exp(score_full - jnp.max(score_full, axis=-1, keepdims=True))
    weight_full = weight_full / jnp.sum(weight_full, axis=-1, keepdims=True)
    weight_half = weight_full.astype(jnp.bfloat16)
    attended = product("hqk,khe->qhe", weight_half, value_rows)
    grad_values = product("hqk,qhe->khe", weight_half, grad_rows).astype(jnp.bfloat16)
    grad_weight = product("qhe,khe->hqk", grad_rows, value_rows)
    grad_score = weight_full * (
        grad_weight - jnp.sum(weight_full * grad_weight, axis=-1, keepdims=True)
    )
    grad_score = grad_score.astype(jnp.bfloat16)
    grad_queries = (factor * product("hqk,khe->qhe", grad_score, key_rows)).astype(jnp.bfloat16)
    grad_keys = (factor * product("hqk,qhe->khe", grad_score, query_rows)).astype(jnp.bfloat16)
    return (attended, grad_queries, grad_keys, grad_values)


def cross_document(inputs, tanh_gate):
    query_rows, key_rows, value_rows, grad_rows, cited_slot = inputs
    factor = query_rows.shape[-1] ** (-0.5)
    score_full = factor * product("qhe,khe->hqk", query_rows, key_rows)
    owner_slot = jnp.arange(key_rows.shape[0], dtype=jnp.int32) // LAT
    allowed = owner_slot[None, :] == cited_slot[:, None]
    score_full = jnp.where(allowed[None], score_full, NEG_FILL)
    weight_full = jnp.exp(score_full - jnp.max(score_full, axis=-1, keepdims=True))
    weight_full = weight_full / jnp.sum(weight_full, axis=-1, keepdims=True)
    present = (cited_slot >= 0)[None, :, None]
    weight_full = jnp.where(present, weight_full, 0.0)
    weight_half = weight_full.astype(jnp.bfloat16)
    attended = product("hqk,khe->qhe", weight_half, value_rows)
    grad_gated = (grad_rows.astype(jnp.float32) * tanh_gate).astype(jnp.bfloat16)
    grad_values = product("hqk,qhe->khe", weight_half, grad_gated).astype(jnp.bfloat16)
    grad_weight = product("qhe,khe->hqk", grad_gated, value_rows)
    grad_score = weight_full * (
        grad_weight - jnp.sum(weight_full * grad_weight, axis=-1, keepdims=True)
    )
    grad_score = grad_score.astype(jnp.bfloat16)
    grad_queries = (factor * product("hqk,khe->qhe", grad_score, key_rows)).astype(jnp.bfloat16)
    grad_keys = (factor * product("hqk,qhe->khe", grad_score, query_rows)).astype(jnp.bfloat16)
    gate_terms = jnp.sum(grad_rows.astype(jnp.float32) * attended, axis=0)
    return (attended, grad_queries, grad_keys, grad_values, gate_terms)


def per_device(q_self, k_self, v_self, q_cross, latents, media, gate, cotangent):
    seq_count = lax.axis_size("seq")
    tok_rows = q_self.shape[1]
    width = q_self.shape[2]
    head_width = width // seq_count
    heads_here = head_width // E
    slot_count = latents.shape[1]
    length = tok_rows * seq_count
    doc_count = length // DOC_LEN
    key_count = MEDIA * LAT

    def to_heads_layout(tensor):
        return tensor[0].reshape(tok_rows, seq_count, head_width)

    latent_rows = latents[0].reshape(slot_count * 2 * LAT, seq_count, head_width)

    def by_document(tensor):
        return tensor.reshape(doc_count, DOC_LEN, heads_here, E)

    def tokens_layout(tensor):
        return tensor.reshape(seq_count, tok_rows, 1, head_width)

    def tokens_out(tensor):
        return tensor.reshape(1, tok_rows, width)

    citations = lax.all_gather(media, "seq", axis=1, tiled=True)
    cited_slot = citations.reshape(doc_count, DOC_LEN)
    slot_base = MEDIA * jnp.arange(doc_count, dtype=jnp.int32)[:, None]
    cited_slot = jnp.where(cited_slot >= 0, cited_slot - slot_base, -1)
    head_start = lax.axis_index("seq") * head_width
    tanh_gate = jnp.tanh(lax.dynamic_slice_in_dim(gate, head_start, head_width, 0)).reshape(
        heads_here, E
    )
    query_heads, key_heads, value_heads, cross_heads, grad_heads, latent_heads = (
        lax.all_to_all(to_heads_layout(q_self), "seq", split_axis=1, concat_axis=0, tiled=True),
        lax.all_to_all(to_heads_layout(k_self), "seq", split_axis=1, concat_axis=0, tiled=True),
        lax.all_to_all(to_heads_layout(v_self), "seq", split_axis=1, concat_axis=0, tiled=True),
        lax.all_to_all(to_heads_layout(q_cross), "seq", split_axis=1, concat_axis=0, tiled=True),
        lax.all_to_all(to_heads_layout(cotangent), "seq", split_axis=1, concat_axis=0, tiled=True),
        lax.all_to_all(latent_rows, "seq", split_axis=1, concat_axis=0, tiled=True),
    )
    grouped = latent_heads.reshape(doc_count, MEDIA, 2, LAT, heads_here, E)
    key_parts = grouped[:, :, 0].reshape(doc_count, key_count, heads_here, E)
    value_parts = grouped[:, :, 1].reshape(doc_count, key_count, heads_here, E)
    cross_parts = lax.map(
        lambda doc_inputs: cross_document(doc_inputs, tanh_gate),
        (by_document(cross_heads), key_parts, value_parts, by_document(grad_heads), cited_slot),
    )
    self_parts = lax.map(
        self_document,
        (
            by_document(query_heads),
            by_document(key_heads),
            by_document(value_heads),
            by_document(grad_heads),
        ),
    )
    mixed_heads = (self_parts[0] + tanh_gate * cross_parts[0]).astype(jnp.bfloat16)
    stacked = jnp.stack(
        [
            cross_parts[2].reshape(doc_count, MEDIA, LAT, heads_here, E),
            cross_parts[3].reshape(doc_count, MEDIA, LAT, heads_here, E),
        ],
        axis=2,
    )
    returned = (
        lax.all_to_all(tokens_layout(mixed_heads), "seq", split_axis=0, concat_axis=2, tiled=True),
        lax.all_to_all(
            tokens_layout(self_parts[1]), "seq", split_axis=0, concat_axis=2, tiled=True
        ),
        lax.all_to_all(
            tokens_layout(self_parts[2]), "seq", split_axis=0, concat_axis=2, tiled=True
        ),
        lax.all_to_all(
            tokens_layout(self_parts[3]), "seq", split_axis=0, concat_axis=2, tiled=True
        ),
        lax.all_to_all(
            tokens_layout(cross_parts[1]), "seq", split_axis=0, concat_axis=2, tiled=True
        ),
        lax.all_to_all(
            stacked.reshape(seq_count, slot_count * 2 * LAT, 1, head_width),
            "seq",
            split_axis=0,
            concat_axis=2,
            tiled=True,
        ),
    )
    mixed_back, grad_query, grad_key, grad_value, grad_cross, grad_latent = returned
    gate_local = (jnp.sum(cross_parts[4], axis=0) * (1.0 - tanh_gate * tanh_gate)).reshape(
        head_width
    )
    padded = lax.dynamic_update_slice_in_dim(
        jnp.zeros((width,), jnp.float32), gate_local, head_start, 0
    )
    gate_grad = lax.psum(padded, ("seq", "doc"))
    latent_out = grad_latent.reshape(1, slot_count, 2, LAT, width)
    return (
        tokens_out(mixed_back),
        tokens_out(grad_query),
        tokens_out(grad_key),
        tokens_out(grad_value),
        tokens_out(grad_cross),
        latent_out,
        gate_grad,
    )


def solution(mesh):
    in_specs = (
        P("doc", "seq", None),
        P("doc", "seq", None),
        P("doc", "seq", None),
        P("doc", "seq", None),
        P("doc", "seq", None, None, None),
        P("doc", "seq"),
        P(),
        P("doc", "seq", None),
    )
    out_specs = (
        P("doc", "seq", None),
        P("doc", "seq", None),
        P("doc", "seq", None),
        P("doc", "seq", None),
        P("doc", "seq", None),
        P("doc", "seq", None, None, None),
        P(),
    )
    return jax.shard_map(
        per_device, mesh=mesh, in_specs=in_specs, out_specs=out_specs, check_vma=False
    )
```

profile of v0, /device:TPU:1, one launch (start us, length us, event | category | flops | bytes accessed | tf_op | source)
XLA Modules:
  0.0 511.9 jit_solution(1290089166003936900)
XLA Ops:
  0.6 2.4 copy.114
  3.0 8.6 %all-to-all-start = ((bf16[128,32,128]{0,2,1:T(8,128)(2,1)}), bf16[128,32,128]{0,2,1:T(8,128)(2,1)S(1)}, u32[]{:S(2)}, u32[]{:S(2)}) async-start(bf16[128,32,128]{0,2,1:T(8,128)(2,1)} %bitcast.38), calls=%async_computation | async-start | bytes 2097152 | tf_op jit(solution)/shard_map/all_to_all | solution.py:103
  12.9 15.6 %all-to-all-done = bf16[128,32,128]{0,2,1:T(8,128)(2,1)S(1)} async-done(((bf16[128,32,128]{0,2,1:T(8,128)(2,1)}), bf16[128,32,128]{0,2,1:T(8,128)(2,1)S(1)}, u32[]{:S(2)}, u32[]{:S(2)}) %all-to-all-start) | async-done | bytes 1048608 | tf_op jit(solution)/shard_map/all_to_all | solution.py:103
  28.5 4.0 all-to-all-start.1
  33.8 15.6 %all-to-all-done.1 = bf16[128,32,128]{0,2,1:T(8,128)(2,1)S(1)} async-done(((bf16[128,32,128]{0,2,1:T(8,128)(2,1)}), bf16[128,32,128]{0,2,1:T(8,128)(2,1)S(1)}, u32[]{:S(2)}, u32[]{:S(2)}) %all-to-all-start.1) | async-done | bytes 1048608 | tf_op jit(solution)/shard_map/all_to_all | solution.py:101
  49.4 4.0 all-to-all-start.2
  53.3 2.3 copy.120
  55.6 14.6 %all-to-all-done.2 = bf16[128,32,128]{0,2,1:T(8,128)(2,1)S(1)} async-done(((bf16[128,32,128]{0,2,1:T(8,128)(2,1)}), bf16[128,32,128]{0,2,1:T(8,128)(2,1)S(1)}, u32[]{:S(2)}, u32[]{:S(2)}) %all-to-all-start.2) | async-done | bytes 1048608 | tf_op jit(solution)/shard_map/all_to_all | solution.py:102
  70.3 4.5 all-to-all-start.3
  77.6 14.1 %all-to-all-done.3 = bf16[128,32,128]{0,2,1:T(8,128)(2,1)} async-done(((bf16[128,32,128]{0,2,1:T(8,128)(2,1)}), bf16[128,32,128]{0,2,1:T(8,128)(2,1)}, u32[]{:S(2)}, u32[]{:S(2)}) %all-to-all-start.3) | async-done | bytes 1048608 | tf_op jit(solution)/shard_map/all_to_all | solution.py:105
  91.7 3.9 all-to-all-start.4
  95.7 29.7 %all_gather.3 = s32[1,4096]{1,0:T(1,128)S(1)} all-gather(s32[1,128]{1,0:T(1,128)S(1)} %copy-done.11), channel_id=1, replica_groups=mesh['seq'=32,'doc'=8] {'seq'}, dimensions={1}, use_global_device_ids=true | all-gather | bytes 16896 | tf_op jit(solution)/shard_map/all_gather | solution.py:92
  126.6 2.3 copy.127
  133.7 2.3 copy.121
  135.9 5.0 all-to-all-start.5
  145.8 78.1 %while.36 = (s32[]{:T(128)}, f32[4,1024,1,128]{3,1,0,2:T(8,128)}, bf16[4,1024,1,128]{3,1,0,2:T(8,128)(2,1)}, bf16[4,1024,1,128]{3,1,0,2:T(8,128)(2,1)}, bf16[4,1...) while((s32[]{:T(128)}, f32[4,1024,1,128]{3,1,0,2:T(8,128)}, ...), condition=%wide.region_4.5_spmd, body=%wide.region_0.4_spmd.sunk | while | flops 1649013760 | bytes 82106536 | solution.py:115
  145.8 1.7 fusion.116
  149.4 1.7 convolution_bitcast_fusion.2
  152.2 3.4 multiply_reduce_fusion.4
  159.1 3.2 fusion.119
  162.5 1.8 fusion.120
  165.3 1.7 fusion.116
  169.0 1.7 convolution_bitcast_fusion.2
  171.7 3.4 multiply_reduce_fusion.4
  178.7 3.2 fusion.119
  182.0 1.8 fusion.120
  184.8 1.7 fusion.116
  188.5 1.7 convolution_bitcast_fusion.2
  191.3 3.4 multiply_reduce_fusion.4
  198.2 3.2 fusion.119
  201.6 1.8 fusion.120
  204.3 1.7 fusion.116
  208.0 1.7 convolution_bitcast_fusion.2
  210.8 3.4 multiply_reduce_fusion.4
  217.7 3.2 fusion.119
  221.0 1.8 fusion.120
  223.8 2.3 fusion.78
  226.1 2.3 copy.128
  231.0 62.0 %while.37 = (s32[]{:T(128)}, f32[4,1024,1,128]{3,1,0,2:T(8,128)}, bf16[4,1024,1,128]{3,1,0,2:T(8,128)(2,1)}, bf16[4,512,1,128]{3,1,0,2:T(8,128)(2,1)}, bf16[4,51...) while((s32[]{:T(128)}, f32[4,1024,1,128]{3,1,0,2:T(8,128)}, ...), condition=%wide.region_10.11_spmd, body=%wide.region_5.10_spmd.sunk | while | flops 820053888 | bytes 29180616 | solution.py:111
  236.5 1.6 multiply_reduce_fusion.5
  238.7 2.0 fusion.130
  249.5 1.5 fusion.129
  252.0 1.6 multiply_reduce_fusion.5
  254.2 2.0 fusion.130
  265.0 1.5 fusion.129
  267.5 1.6 multiply_reduce_fusion.5
  269.7 2.0 fusion.130
  283.0 1.6 multiply_reduce_fusion.5
  285.2 2.0 fusion.130
  293.0 2.4 add_convert_fusion
  295.4 24.3 %all_to_all.180 = bf16[32,128,1,128]{3,1,2,0:T(8,128)(2,1)} all-to-all(bf16[32,128,1,128]{3,1,2,0:T(8,128)(2,1)S(1)} %bitcast.321), channel_id=1, replica_groups=mesh['seq'=32,'doc'=8] {'seq'}, dimensions={0} | all-to-all | bytes 2097152 | tf_op jit(solution)/shard_map/all_to_all | solution.py:133
  319.8 20.9 %all_to_all.181 = bf16[32,128,1,128]{3,1,2,0:T(8,128)(2,1)} all-to-all(bf16[32,128,1,128]{3,1,2,0:T(8,128)(2,1)S(1)} %bitcast.311), channel_id=1, replica_groups=mesh['seq'=32,'doc'=8] {'seq'}, dimensions={0} | all-to-all | bytes 2097152 | tf_op jit(solution)/shard_map/all_to_all | solution.py:134
  340.7 20.7 %all_to_all.182 = bf16[32,128,1,128]{3,1,2,0:T(8,128)(2,1)S(1)} all-to-all(bf16[32,128,1,128]{3,1,2,0:T(8,128)(2,1)S(1)} %bitcast.312), channel_id=1, replica_groups=mesh['seq'=32,'doc'=8] {'seq'}, dimensions={0} | all-to-all | bytes 2097152 | tf_op jit(solution)/shard_map/all_to_all | solution.py:137
  361.3 20.7 %all_to_all.183 = bf16[32,128,1,128]{3,1,2,0:T(8,128)(2,1)S(1)} all-to-all(bf16[32,128,1,128]{3,1,2,0:T(8,128)(2,1)S(1)} %bitcast.313), channel_id=1, replica_groups=mesh['seq'=32,'doc'=8] {'seq'}, dimensions={0} | all-to-all | bytes 2097152 | tf_op jit(solution)/shard_map/all_to_all | solution.py:140
  382.0 4.0 all-to-all-start.10
  388.3 14.5 %all-to-all-done.10 = bf16[32,128,1,128]{3,1,2,0:T(8,128)(2,1)S(1)} async-done(((bf16[32,128,1,128]{3,1,2,0:T(8,128)(2,1)}), bf16[32,128,1,128]{3,1,2,0:T(8,128)(2,1)S(1)}, u32[]{:S(2)}, u32[]{:S(2)}) %all-to-all-start.10) | async-done | bytes 1048608 | tf_op jit(solution)/shard_map/all_to_all | solution.py:143
  402.9 4.5 all-to-all-start.11
  408.2 83.9 %psum.7 = f32[4096]{0:T(1024)} all-reduce(f32[4096]{0:T(1024)S(1)} %multiply_dynamic-update-slice_fusion), channel_id=1, replica_groups=mesh['seq'=32,'doc'=8] {'seq','doc'}, use_global_device_ids=true, to_apply=%region_12.13 | all-reduce | flops 4096 | bytes 32768 | tf_op jit(solution)/shard_map/psum | solution.py:161
  492.2 2.3 copy.136
  494.4 2.3 copy.154
  496.7 2.3 copy.139
  499.0 2.3 copy.155
  502.5 2.3 copy.156
  508.8 1.9 copy.153
  (192 shorter events, 103.7 us)
Async XLA Ops:
  0.6 11.0 %copy-start.9 = (bf16[1,128,4096]{2,1,0:T(8,128)(2,1)S(1)}, bf16[1,128,4096]{2,1,0:T(8,128)(2,1)}, u32[]{:S(2)}) copy-start(bf16[1,128,4096]{2,1,0:T(8,128)(2,1)} %param.12) | copy-start | bytes 3145732
  3.0 25.5 %all-to-all-start = ((bf16[128,32,128]{0,2,1:T(8,128)(2,1)}), bf16[128,32,128]{0,2,1:T(8,128)(2,1)S(1)}, u32[]{:S(2)}, u32[]{:S(2)}) async-start(bf16[128,32,128]{0,2,1:T(8,128)(2,1)} %bitcast.38), calls=%async_computation | async-start | bytes 2097152 | tf_op jit(solution)/shard_map/all_to_all | solution.py:103
  12.9 19.6 %copy-start.10 = (bf16[1,128,4096]{2,1,0:T(8,128)(2,1)S(1)}, bf16[1,128,4096]{2,1,0:T(8,128)(2,1)}, u32[]{:S(2)}) copy-start(bf16[1,128,4096]{2,1,0:T(8,128)(2,1)} %param.13) | copy-start | bytes 3145732
  28.5 20.9 %all-to-all-start.1 = ((bf16[128,32,128]{0,2,1:T(8,128)(2,1)}), bf16[128,32,128]{0,2,1:T(8,128)(2,1)S(1)}, u32[]{:S(2)}, u32[]{:S(2)}) async-start(bf16[128,32,128]{0,2,1:T(8,128)(2,1)} %bitcast.43), calls=%async_computation.1 | async-start | bytes 2097152 | tf_op jit(solution)/shard_map/all_to_all | solution.py:101
  49.4 20.9 %all-to-all-start.2 = ((bf16[128,32,128]{0,2,1:T(8,128)(2,1)}), bf16[128,32,128]{0,2,1:T(8,128)(2,1)S(1)}, u32[]{:S(2)}, u32[]{:S(2)}) async-start(bf16[128,32,128]{0,2,1:T(8,128)(2,1)} %bitcast.314), calls=%async_computation.2 | async-start | bytes 2097152 | tf_op jit(solution)/shard_map/all_to_all | solution.py:102
  70.3 5.9 %copy-start.4 = (bf16[128,32,128]{0,2,1:T(8,128)(2,1)}, bf16[128,32,128]{0,2,1:T(8,128)(2,1)S(1)}, u32[]{:S(2)}) copy-start(bf16[128,32,128]{0,2,1:T(8,128)(2,1)S(1)} %all-to-all-done.2) | copy-start | bytes 3145732
  70.3 21.4 %all-to-all-start.3 = ((bf16[128,32,128]{0,2,1:T(8,128)(2,1)}), bf16[128,32,128]{0,2,1:T(8,128)(2,1)}, u32[]{:S(2)}, u32[]{:S(2)}) async-start(bf16[128,32,128]{0,2,1:T(8,128)(2,1)} %bitcast.310), calls=%async_computation.3 | async-start | bytes 2097152 | tf_op jit(solution)/shard_map/all_to_all | solution.py:105
  76.2 19.5 %copy-start.11 = (s32[1,128]{1,0:T(1,128)S(1)}, s32[1,128]{1,0:T(1,128)}, u32[]{:S(2)}) copy-start(s32[1,128]{1,0:T(1,128)} %param.17) | copy-start | bytes 1540
  91.7 44.2 %all-to-all-start.4 = ((bf16[128,32,128]{2,0,1:T(8,128)(2,1)}), bf16[128,32,128]{2,0,1:T(8,128)(2,1)S(1)}, u32[]{:S(2)}, u32[]{:S(2)}) async-start(bf16[128,32,128]{2,0,1:T(8,128)(2,1)} %copy.126), calls=%async_computation.4 | async-start | bytes 2097152 | tf_op jit(solution)/shard_map/all_to_all | solution.py:106
  131.0 1.3 copy-start.5
  135.9 6.5 %copy-start.3 = (bf16[128,32,128]{2,0,1:T(8,128)(2,1)}, bf16[128,32,128]{2,0,1:T(8,128)(2,1)S(1)}, u32[]{:S(2)}) copy-start(bf16[128,32,128]{2,0,1:T(8,128)(2,1)S(1)} %all-to-all-done.4) | copy-start | bytes 3145732
  135.9 90.2 %all-to-all-start.5 = ((bf16[128,32,128]{0,2,1:T(8,128)(2,1)}), bf16[128,32,128]{0,2,1:T(8,128)(2,1)}, u32[]{:S(2)}, u32[]{:S(2)}) async-start(bf16[128,32,128]{0,2,1:T(8,128)(2,1)} %bitcast.63), calls=%async_computation.5 | async-start | bytes 2097152 | tf_op jit(solution)/shard_map/all_to_all | solution.py:104
  147.5 1.9 copy-start
  152.2 3.6 copy-start.1
  167.0 1.9 copy-start
  171.7 3.6 copy-start.1
  186.6 1.9 copy-start
  191.3 3.6 copy-start.1
  206.1 1.9 copy-start
  210.8 3.6 copy-start.1
  232.1 4.5 copy-start.2
  247.6 4.5 copy-start.2
  263.1 4.5 copy-start.2
  278.6 4.5 copy-start.2
  295.4 24.4 %copy-start.6 = (bf16[4,1024,1,128]{3,1,0,2:T(8,128)(2,1)S(1)}, bf16[4,1024,1,128]{3,1,0,2:T(8,128)(2,1)}, u32[]{:S(2)}) copy-start(bf16[4,1024,1,128]{3,1,0,2:T(8,128)(2,1)} %get-tuple-element.213) | copy-start | bytes 3145732
  295.4 45.2 %copy-start.7 = (bf16[4,1024,1,128]{3,1,0,2:T(8,128)(2,1)S(1)}, bf16[4,1024,1,128]{3,1,0,2:T(8,128)(2,1)}, u32[]{:S(2)}) copy-start(bf16[4,1024,1,128]{3,1,0,2:T(8,128)(2,1)} %get-tuple-element.214) | copy-start | bytes 3145732
  319.8 41.6 %copy-start.8 = (bf16[4,1024,1,128]{3,1,0,2:T(8,128)(2,1)S(1)}, bf16[4,1024,1,128]{3,1,0,2:T(8,128)(2,1)}, u32[]{:S(2)}) copy-start(bf16[4,1024,1,128]{3,1,0,2:T(8,128)(2,1)} %get-tuple-element.215) | copy-start | bytes 3145732
  382.0 20.9 %all-to-all-start.10 = ((bf16[32,128,1,128]{3,1,2,0:T(8,128)(2,1)}), bf16[32,128,1,128]{3,1,2,0:T(8,128)(2,1)S(1)}, u32[]{:S(2)}, u32[]{:S(2)}) async-start(bf16[32,128,1,128]{3,1,2,0:T(8,128)(2,1)} %bitcast.309), calls=%async_computation.10 | async-start | bytes 2097152 | tf_op jit(solution)/shard_map/all_to_all | solution.py:143
  402.9 105.9 %all-to-all-start.11 = ((bf16[32,128,1,128]{3,1,2,0:T(8,128)(2,1)}), bf16[32,128,1,128]{3,1,2,0:T(8,128)(2,1)}, u32[]{:S(2)}, u32[]{:S(2)}) async-start(bf16[32,128,1,128]{3,1,2,0:T(8,128)(2,1)} %bitcast.308), calls=%async_computation.11 | async-start | bytes 2097152 | tf_op jit(solution)/shard_map/all_to_all | solution.py:146
where the time goes:
time: 515 us; the launch traced here: 512 us
  blocking collectives  200 us (39%)
  local copies, waits for them, and re-layouts  91.4 us (18%)
  matrix products  90.8 us (18%)
  waiting for transfers between devices  74.5 us (14%)
  starting transfers between devices  38.3 us (7%)
  other arithmetic  15.1 us (3%)
    dot_general x48, matrix products, product(): return jnp.einsum(form, left, right, preferred_element_type=jnp.float32)  90.8 us
    psum x1, blocking collectives, per_device(): gate_grad = lax.psum(padded, ('seq', 'doc'))  83.9 us
    all_gather x1, blocking collectives, per_device(): citations = lax.all_gather(media, 'seq', axis=1, tiled=True)  29.7 us
    dynamic_update_slice x60, local copies, waits for them, and re-layouts, per_device(): lax.map(lambda doc_inputs: cross_document(doc_inputs, tanh_gate), (by_doc...  27.8 us
    all_to_all x1, blocking collectives, per_device(): lax.all_to_all(tokens_layout(mixed_heads), 'seq', split_axis=0, concat_ax...  24.3 us
    all_to_all x1, blocking collectives, per_device(): lax.all_to_all(tokens_layout(self_parts[1]), 'seq', split_axis=0, concat_...  20.9 us
    all_to_all x1, blocking collectives, per_device(): lax.all_to_all(tokens_layout(self_parts[2]), 'seq', split_axis=0, concat_...  20.7 us
    all_to_all x1, blocking collectives, per_device(): lax.all_to_all(tokens_layout(self_parts[3]), 'seq', split_axis=0, concat_...  20.7 us
  transfers between devices with their start and end apart: 8, of which 5 were waited for; matrix products, arithmetic and copies ran while one was open for 23% of the time, Pallas kernels for 0%

commit v1 on v0

v1 whole, which is shorter than its diff:
```python
import functools

import jax
import jax.numpy as jnp
from jax import lax
from jax.experimental import pallas as pl
from jax.experimental.pallas import tpu as pltpu
from jax.sharding import PartitionSpec as P

E = 128
LAT = 64
GROUP = 8
ROWS = 128
DOC = GROUP * ROWS
HEADS = 4
COLS = HEADS * E
KEYS = GROUP * LAT
BLOCK = 256
WIDTH = GROUP * COLS
SCALE = E**-0.5
NEG_FILL = -1e30
MESH = pl.DeviceIdType.MESH
F32 = jnp.float32
BF16 = jnp.bfloat16


def dot(left, right, left_dim, right_dim):
    return lax.dot_general(
        left, right, (((left_dim,), (right_dim,)), ((), ())), preferred_element_type=F32
    )


def softmax_and_grad(scores, weights_grad_of, inverse_of):
    peak = jnp.max(scores, axis=0, keepdims=True)
    weights = jnp.exp(SCALE * (scores - peak))
    weights = weights * inverse_of(jnp.sum(weights, axis=0, keepdims=True))
    half = weights.astype(BF16)
    weights_grad = weights_grad_of()
    inner = jnp.sum(weights * weights_grad, axis=0, keepdims=True)
    return half, (weights * (weights_grad - inner)).astype(BF16)


def cross_head(head, gate_row, media_row, qc_buf, cot_buf, lat_buf, mixed, gqc_buf, glat_buf, acc_k, acc_v):
    cols = pl.ds(pl.multiple_of(head * E, E), E)
    keys = lat_buf[:, 0, :, cols].reshape(KEYS, E)
    values = lat_buf[:, 1, :, cols].reshape(KEYS, E)
    tanh_gate = jnp.tanh(gate_row)
    slot = lax.broadcasted_iota(jnp.int32, (KEYS, BLOCK), 0) // LAT
    acc_k[pl.ds(0, KEYS), :] = jnp.zeros((KEYS, E), F32)
    acc_v[pl.ds(0, KEYS), :] = jnp.zeros((KEYS, E), F32)

    def step(i, gate_sum):
        rows = pl.ds(pl.multiple_of(i * BLOCK, BLOCK), BLOCK)
        cited = media_row(i)
        queries = qc_buf[rows, cols]
        cot = cot_buf[rows, cols].astype(F32)
        cot_cross = (cot * tanh_gate).astype(BF16)
        scores = dot(keys, queries, 1, 1)
        scores = jnp.where(slot == cited, scores, NEG_FILL)
        half, scores_grad = softmax_and_grad(
            scores,
            lambda: dot(values, cot_cross, 1, 1),
            lambda total: jnp.where(cited >= 0, 1.0 / total, 0.0),
        )
        out = dot(values, half, 0, 0).T
        mixed[rows, cols] = tanh_gate * out
        acc_v[pl.ds(0, KEYS), :] += dot(half, cot_cross, 1, 0)
        gqc_buf[rows, cols] = (SCALE * dot(keys, scores_grad, 0, 0)).T.astype(BF16)
        acc_k[pl.ds(0, KEYS), :] += dot(scores_grad, queries, 1, 0)
        return gate_sum + jnp.sum(cot * out, axis=0, keepdims=True)

    gate_sum = lax.fori_loop(0, DOC // BLOCK, step, jnp.zeros((1, E), F32))
    glat_buf[:, 0, :, cols] = (SCALE * acc_k[pl.ds(0, KEYS), :]).astype(BF16).reshape(GROUP, LAT, E)
    glat_buf[:, 1, :, cols] = acc_v[pl.ds(0, KEYS), :].astype(BF16).reshape(GROUP, LAT, E)
    return gate_sum * (1.0 - tanh_gate * tanh_gate)


def self_head(head, q_buf, k_buf, v_buf, cot_buf, mixed, out_buf, gq_buf, gk_buf, gv_buf, acc_k, acc_v):
    cols = pl.ds(pl.multiple_of(head * E, E), E)
    acc_k[...] = jnp.zeros((DOC, E), F32)
    acc_v[...] = jnp.zeros((DOC, E), F32)
    for i in range(DOC // BLOCK):
        rows = pl.ds(i * BLOCK, BLOCK)
        seen = pl.ds(0, (i + 1) * BLOCK)
        queries = q_buf[rows, cols]
        cot = cot_buf[rows, cols]
        keys = k_buf[seen, cols]
        values = v_buf[seen, cols]
        scores = dot(keys, queries, 1, 1)
        shape = scores.shape
        causal = lax.broadcasted_iota(jnp.int32, shape, 0) <= i * BLOCK + lax.broadcasted_iota(jnp.int32, shape, 1)
        scores = jnp.where(causal, scores, -jnp.inf)
        half, scores_grad = softmax_and_grad(
            scores, lambda: dot(values, cot, 1, 1), lambda total: 1.0 / total
        )
        out = dot(values, half, 0, 0).T
        out_buf[rows, cols] = (out + mixed[rows, cols]).astype(BF16)
        acc_v[seen, :] += dot(half, cot, 1, 0)
        gq_buf[rows, cols] = (SCALE * dot(keys, scores_grad, 0, 0)).T.astype(BF16)
        acc_k[seen, :] += dot(scores_grad, queries, 1, 0)
    gk_buf[:, cols] = (SCALE * acc_k[...]).astype(BF16)
    gv_buf[:, cols] = acc_v[...].astype(BF16)


def kernel(
    x_count, z_count,
    q_ref, k_ref, v_ref, qc_ref, lat_ref, cot_ref, media_ref, gate_ref,
    out_ref, gq_ref, gk_ref, gv_ref, gqc_ref, glat_ref, gate_out_ref,
    q_buf, k_buf, v_buf, qc_buf, cot_buf, lat_buf, media_buf,
    out_buf, gq_buf, gk_buf, gv_buf, gqc_buf, glat_buf,
    mixed, acc_k, acc_v, gate_own, gate_x, gate_z, gate_all,
    in_send, in_recv, out_send, out_recv, gx_send, gx_recv, gz_send, gz_recv, gg_send, gg_recv,
):
    seq = lax.axis_index("seq")
    doc = lax.axis_index("doc")
    x = seq // GROUP
    me = lax.rem(seq, GROUP)

    def in_group(k):
        rank = lax.rem(me + k, GROUP)
        return rank, {"seq": x * GROUP + rank}

    def along_x(k):
        return {"seq": lax.rem(x + k, x_count) * GROUP + me}

    def along_z(k):
        return {"doc": lax.rem(doc + k, z_count)}

    barrier = pltpu.get_barrier_semaphore()

    def greet(device):
        pl.semaphore_signal(barrier, inc=1, device_id=device, device_id_type=MESH)

    def greet_group(k, c):
        greet(in_group(k)[1])
        return c

    def greet_z(k, c):
        greet(along_z(k))
        return c

    def greet_x(k, c):
        greet(along_x(k))
        return c

    lax.fori_loop(1, GROUP, greet_group, 0)
    lax.fori_loop(1, x_count, greet_x, 0)
    lax.fori_loop(1, z_count, greet_z, 0)
    pl.semaphore_wait(barrier, GROUP - 1 + x_count - 1 + z_count - 1)

    own_rows = pl.ds(pl.multiple_of(me * ROWS, ROWS), ROWS)
    own_cols = pl.ds(pl.multiple_of(me * COLS, COLS), COLS)

    def in_views(t, rank):
        cols = pl.ds(pl.multiple_of(rank * COLS, COLS), COLS)
        if t == 0:
            return media_ref, media_buf.at[me]
        if t == 1:
            return lat_ref.at[0, 0, :, :, cols], lat_buf.at[me]
        ref, buf = {2: (cot_ref, cot_buf), 3: (qc_ref, qc_buf), 4: (k_ref, k_buf), 5: (q_ref, q_buf), 6: (v_ref, v_buf)}[t]
        return ref.at[0, :, cols], buf.at[own_rows]

    for part in ((0, 1, 2, 3), (4, 5, 6)):
        for t in part:
            src, dst = in_views(t, me)
            pltpu.make_async_copy(src, dst, in_recv.at[t]).start()

        def send(k, c, part=part):
            rank, device = in_group(k)
            for t in part:
                src, dst = in_views(t, rank)
                pltpu.make_async_remote_copy(
                    src_ref=src, dst_ref=dst, send_sem=in_send.at[t], recv_sem=in_recv.at[t],
                    device_id=device, device_id_type=MESH,
                ).start()
            return c

        lax.fori_loop(1, GROUP, send, 0)

    def await_bytes(ref, sem):
        pltpu.make_async_copy(ref, ref, sem).wait()

    in_bufs = (media_buf, lat_buf, cot_buf, qc_buf, k_buf, q_buf, v_buf)

    def out_views(t, head, rank):
        there = pl.ds(pl.multiple_of(me * COLS + head * E, E), E)
        here = pl.ds(pl.multiple_of(head * E, E), E)
        if t == 5:
            return glat_buf.at[rank, :, :, here], glat_ref.at[0, 0, :, :, there]
        ref, buf = ((out_ref, out_buf), (gq_ref, gq_buf), (gk_ref, gk_buf), (gv_ref, gv_buf), (gqc_ref, gqc_buf))[t]
        return buf.at[pl.ds(pl.multiple_of(rank * ROWS, ROWS), ROWS), here], ref.at[0, :, there]

    def send_out(head, part):
        for t in part:
            src, dst = out_views(t, head, me)
            pltpu.make_async_copy(src, dst, out_recv.at[t, head]).start()

        def send(k, c):
            rank, device = in_group(k)
            for t in part:
                src, dst = out_views(t, head, rank)
                pltpu.make_async_remote_copy(
                    src_ref=src, dst_ref=dst, send_sem=out_send.at[t, head], recv_sem=out_recv.at[t, head],
                    device_id=device, device_id_type=MESH,
                ).start()
            return c

        lax.fori_loop(1, GROUP, send, 0)

    for t in (0, 1, 2, 3):
        await_bytes(in_bufs[t], in_recv.at[t])
    first_slot = x * GROUP

    def media_row(i):
        pair = jnp.concatenate([media_buf[2 * i], media_buf[2 * i + 1]], axis=1)
        return jnp.where(pair >= 0, pair - first_slot, -1)

    def cross_step(head, c):
        gate_row = gate_ref[pl.ds(me * HEADS + head, 1), :]
        gate_own[pl.ds(head, 1), :] = cross_head(
            head, gate_row, media_row, qc_buf, cot_buf, lat_buf, mixed, gqc_buf, glat_buf, acc_k, acc_v
        )
        send_out(head, (4, 5))
        return c

    lax.fori_loop(0, HEADS, cross_step, 0)

    gate_x[x] = gate_own[...]

    def send_x(k, c):
        pltpu.make_async_remote_copy(
            src_ref=gate_own, dst_ref=gate_x.at[x], send_sem=gx_send.at[k], recv_sem=gx_recv.at[k],
            device_id=along_x(k), device_id_type=MESH,
        ).start()
        return c

    lax.fori_loop(1, x_count, send_x, 0)

    for t in (4, 5, 6):
        await_bytes(in_bufs[t], in_recv.at[t])

    def self_step(head, c):
        self_head(head, q_buf, k_buf, v_buf, cot_buf, mixed, out_buf, gq_buf, gk_buf, gv_buf, acc_k, acc_v)
        send_out(head, (0, 1, 2, 3))
        return c

    lax.fori_loop(0, HEADS, self_step, 0)

    def wait_x(k, c):
        pltpu.make_async_remote_copy(
            src_ref=gate_own, dst_ref=gate_x.at[x], send_sem=gx_send.at[k], recv_sem=gx_recv.at[k],
            device_id=along_x(k), device_id_type=MESH,
        ).wait()
        return c

    lax.fori_loop(1, x_count, wait_x, 0)
    gate_own[...] = jnp.sum(gate_x[...], axis=0)
    gate_z[doc] = gate_own[...]

    def copy_z(k):
        return pltpu.make_async_remote_copy(
            src_ref=gate_own, dst_ref=gate_z.at[doc], send_sem=gz_send.at[k], recv_sem=gz_recv.at[k],
            device_id=along_z(k), device_id_type=MESH,
        )

    def send_z(k, c):
        copy_z(k).start()
        return c

    def wait_z(k, c):
        copy_z(k).wait()
        return c

    lax.fori_loop(1, z_count, send_z, 0)
    lax.fori_loop(1, z_count, wait_z, 0)
    gate_own[...] = jnp.sum(gate_z[...], axis=0)
    gate_all[me] = gate_own[...]

    def copy_group(k):
        return pltpu.make_async_remote_copy(
            src_ref=gate_own, dst_ref=gate_all.at[me], send_sem=gg_send.at[k], recv_sem=gg_recv.at[k],
            device_id=in_group(k)[1], device_id_type=MESH,
        )

    def send_group(k, c):
        copy_group(k).start()
        return c

    def wait_group(k, c):
        copy_group(k).wait()
        return c

    lax.fori_loop(1, GROUP, send_group, 0)
    lax.fori_loop(1, GROUP, wait_group, 0)
    for rank in range(GROUP):
        gate_out_ref[pl.ds(rank * HEADS, HEADS), :] = gate_all[rank, pl.ds(0, HEADS), :]

    most = GROUP - 1
    for t, buf in enumerate(in_bufs):
        await_bytes(buf.at[pl.ds(0, most * (buf.shape[0] // GROUP))], in_send.at[t])

    def end(head, c):
        here = pl.ds(pl.multiple_of(head * E, E), E)
        for t, buf in enumerate((out_buf, gq_buf, gk_buf, gv_buf, gqc_buf)):
            await_bytes(buf.at[pl.ds(0, most * ROWS), here], out_send.at[t, head])
            await_bytes(buf.at[:, here], out_recv.at[t, head])
        await_bytes(glat_buf.at[pl.ds(0, most), :, :, here], out_send.at[5, head])
        await_bytes(glat_buf.at[:, :, :, here], out_recv.at[5, head])
        return c

    lax.fori_loop(0, HEADS, end, 0)


def finish_kernel(*refs):
    count = len(refs) // 2
    sems = refs[-1]
    copies = [pltpu.make_async_copy(refs[i], refs[count + i], sems.at[i]) for i in range(count)]
    for copy in copies:
        copy.start()
    for copy in copies:
        copy.wait()


def per_device(x_count, z_count, q, k, v, qc, lat, media, gate, cot):
    any_space = pl.BlockSpec(memory_space=pl.ANY)
    vmem = pl.BlockSpec(memory_space=pltpu.VMEM)
    token = jax.ShapeDtypeStruct((1, ROWS, WIDTH), BF16)
    outs = (token,) * 5 + (jax.ShapeDtypeStruct(lat.shape, BF16),)
    tokens = pltpu.VMEM((DOC, COLS), BF16)
    latents = pltpu.VMEM((GROUP, 2, LAT, COLS), BF16)
    dma = pltpu.SemaphoreType.DMA
    results = pl.pallas_call(
        functools.partial(kernel, x_count, z_count),
        name="attention",
        out_shape=outs + (jax.ShapeDtypeStruct((GROUP * HEADS, E), F32),),
        in_specs=[any_space] * 7 + [vmem],
        out_specs=[any_space] * 6 + [vmem],
        scratch_shapes=[
            tokens, tokens, tokens, tokens, tokens, latents, pltpu.VMEM((GROUP, 1, ROWS), jnp.int32),
            tokens, tokens, tokens, tokens, tokens, latents,
            pltpu.VMEM((DOC, COLS), F32), pltpu.VMEM((DOC, E), F32), pltpu.VMEM((DOC, E), F32),
            pltpu.VMEM((8, E), F32), pltpu.VMEM((x_count, 8, E), F32),
            pltpu.VMEM((z_count, 8, E), F32), pltpu.VMEM((GROUP, 8, E), F32),
            dma((7,)), dma((7,)), dma((6, HEADS)), dma((6, HEADS)),
            dma((x_count,)), dma((x_count,)), dma((z_count,)), dma((z_count,)), dma((GROUP,)), dma((GROUP,)),
        ],
        compiler_params=pltpu.CompilerParams(
            collective_id=0, has_side_effects=True, vmem_limit_bytes=48 << 20
        ),
    )(q, k, v, qc, lat, cot, media, gate.reshape(GROUP * HEADS, E))
    done = pl.pallas_call(
        finish_kernel,
        name="finish",
        out_shape=outs,
        in_specs=[any_space] * 6,
        out_specs=[any_space] * 6,
        scratch_shapes=[dma((6,))],
    )(*results[:6])
    return (*done, results[6].reshape(WIDTH))


def solution(mesh):
    token = P("doc", "seq", None)
    latent = P("doc", "seq", None, None, None)
    return jax.shard_map(
        functools.partial(per_device, mesh.shape["seq"] // GROUP, mesh.shape["doc"]),
        mesh=mesh,
        in_specs=(token, token, token, token, latent, P("doc", "seq"), P(), token),
        out_specs=(token, token, token, token, token, latent, P()),
        check_vma=False,
    )
```

time: 515 us -> 348 us (0.68)
  Pallas kernels: 0 us -> 340 us
  blocking collectives: 200 us -> 0 us
  matrix products: 90.8 us -> 0 us
  local copies, waits for them, and re-layouts: 91.4 us -> 6.93 us
  waiting for transfers between devices: 74.5 us -> 0 us
  starting transfers between devices: 38.3 us -> 0 us
  other arithmetic: 15.1 us -> 0 us
    pallas_call x0 -> x2, Pallas kernels: none -> 340 us  [the longest x1 192 us: per_device(): pl.pallas_call(finish_kernel, name='finish', out_shape=outs, in_specs=[an...]
    dot_general x48 -> x0, matrix products: 90.8 us -> none  [product(): return jnp.einsum(form, left, right, preferred_element_type=jnp.float32)]
    all_to_all x4 -> x0, blocking collectives: 86.5 us -> none  [the longest x1 24.3 us: per_device(): lax.all_to_all(tokens_layout(mixed_heads), 'seq', split_axis=0, concat_ax...]
    psum x1 -> x0, blocking collectives: 83.9 us -> none  [per_device(): gate_grad = lax.psum(padded, ('seq', 'doc'))]
    all_to_all x8 -> x0, waiting for transfers between devices: 74.5 us -> none  [the longest x1 15.6 us: per_device(): lax.all_to_all(to_heads_layout(q_self), 'seq', split_axis=1, concat_axis=...]
    all_to_all x8 -> x0, starting transfers between devices: 38.3 us -> none  [the longest x1 8.59 us: per_device(): lax.all_to_all(to_heads_layout(v_self), 'seq', split_axis=1, concat_axis=...]
    all_gather x1 -> x0, blocking collectives: 29.7 us -> none  [per_device(): citations = lax.all_gather(media, 'seq', axis=1, tiled=True)]
    dynamic_update_slice x60 -> x0, local copies, waits for them, and re-layouts: 27.8 us -> none  [per_device(): lax.map(lambda doc_inputs: cross_document(doc_inputs, tanh_gate), (by_doc...]
  transfers between devices with their start and end apart: 8 -> 0, of which waited for: 5 -> 0; matrix products, arithmetic and copies ran while one was open for 23% -> 0% of each run, Pallas kernels for 0% -> 0%
where the time goes in v1:
time: 348 us
  Pallas kernels  340 us (98%)
  local copies, waits for them, and re-layouts  6.93 us (2%)
    pallas_call x1, Pallas kernels, per_device(): pl.pallas_call(finish_kernel, name='finish', out_shape=outs, in_specs=[an...  192 us
    pallas_call x1, Pallas kernels, per_device(): pl.pallas_call(functools.partial(kernel, x_count, z_count), name='attenti...  149 us

profile of v1, /device:TPU:1, one launch (start us, length us, event | category | flops | bytes accessed | tf_op | source)
XLA Modules:
  0.0 347.9 jit_solution(12007608481914350920)
XLA Ops:
  0.6 0.0 copy-start.6
  0.6 0.6 copy-done.6
  1.3 0.0 copy-start.5
  1.3 0.7 copy-done.5
  2.0 148.5 %attention.1 = (bf16[1,128,4096]{2,1,0:T(8,128)(2,1)S(1)}, bf16[1,128,4096]{2,1,0:T(8,128)(2,1)S(1)}, bf16[1,128,4096]{2,1,0:T(8,128)(2,1)S(1)}, bf16[1,128,4096...) custom-call(bf16[1,128,4096]{2,1,0:T(8,128)(2,1)} %q_ref.1, ...), custom_call_target="tpu_custom_call" | custom-call | tf_op jit(solution)/shard_map/attention/pallas_call | solution.py:332
  150.5 0.0 copy-start
  150.5 1.0 copy-done
  151.6 0.0 copy-start.1
  151.6 1.0 copy-done.1
  152.5 0.0 copy-start.2
  152.5 1.0 copy-done.2
  153.5 0.0 copy-start.3
  153.5 1.0 copy-done.3
  154.5 0.0 copy-start.4
  154.5 1.0 copy-done.4
  155.5 191.7 %finish.1 = (bf16[1,128,4096]{2,1,0:T(8,128)(2,1)}, bf16[1,128,4096]{2,1,0:T(8,128)(2,1)}, bf16[1,128,4096]{2,1,0:T(8,128)(2,1)}, bf16[1,128,4096]{2,1,0:T(8,128...) custom-call(bf16[1,128,4096]{2,1,0:T(8,128)(2,1)} %copy-done, ...), custom_call_target="tpu_custom_call" | custom-call | tf_op jit(solution)/shard_map/finish/pallas_call | solution.py:351
  347.2 0.6 copy.16
Async XLA Ops:
  0.6 0.7 copy-start.6
  1.3 0.7 copy-start.5
  150.5 1.0 copy-start
  151.6 1.0 copy-start.1
  152.5 1.0 copy-start.2
  153.5 1.0 copy-start.3
  154.5 1.0 copy-start.4

commit v2 on v1

--- a/solution.py
+++ b/solution.py
@@ -108,8 +108,8 @@
     out_ref, gq_ref, gk_ref, gv_ref, gqc_ref, glat_ref, gate_out_ref,
     q_buf, k_buf, v_buf, qc_buf, cot_buf, lat_buf, media_buf,
     out_buf, gq_buf, gk_buf, gv_buf, gqc_buf, glat_buf,
-    mixed, acc_k, acc_v, gate_own, gate_x, gate_z, gate_all,
-    in_send, in_recv, out_send, out_recv, gx_send, gx_recv, gz_send, gz_recv, gg_send, gg_recv,
+    mixed, acc_k, acc_v, gate_buf, gate_own, gate_all, gate_sums, gate_in,
+    gate_sem, in_send, in_recv, out_send, out_recv, gather_recv, gate_send, gate_recv, spread_send,
 ):
     seq = lax.axis_index("seq")
     doc = lax.axis_index("doc")
@@ -120,11 +120,14 @@
         rank = lax.rem(me + k, GROUP)
         return rank, {"seq": x * GROUP + rank}
 
-    def along_x(k):
-        return {"seq": lax.rem(x + k, x_count) * GROUP + me}
-
-    def along_z(k):
-        return {"doc": lax.rem(doc + k, z_count)}
+    leads = me == 0
+    group_at = x + x_count * doc
+    stages = (x_count * z_count).bit_length() - 1
+
+    def partner(stage):
+        bit = 1 << stage
+        other = group_at + bit - 2 * bit * lax.rem(group_at // bit, 2)
+        return {"seq": lax.rem(other, x_count) * GROUP, "doc": other // x_count}
 
     barrier = pltpu.get_barrier_semaphore()
 
@@ -135,21 +138,22 @@
         greet(in_group(k)[1])
         return c
 
-    def greet_z(k, c):
-        greet(along_z(k))
-        return c
-
-    def greet_x(k, c):
-        greet(along_x(k))
-        return c
-
     lax.fori_loop(1, GROUP, greet_group, 0)
-    lax.fori_loop(1, x_count, greet_x, 0)
-    lax.fori_loop(1, z_count, greet_z, 0)
-    pl.semaphore_wait(barrier, GROUP - 1 + x_count - 1 + z_count - 1)
+
+    @pl.when(leads)
+    def _():
+        for stage in range(stages):
+            greet(partner(stage))
+        pl.semaphore_wait(barrier, GROUP - 1 + stages)
+
+    @pl.when(jnp.logical_not(leads))
+    def _():
+        pl.semaphore_wait(barrier, GROUP - 1)
 
     own_rows = pl.ds(pl.multiple_of(me * ROWS, ROWS), ROWS)
-    own_cols = pl.ds(pl.multiple_of(me * COLS, COLS), COLS)
+    gate_load = pltpu.make_async_copy(gate_ref, gate_buf, gate_sem)
+    gate_load.start()
+    gate_own[...] = jnp.zeros_like(gate_own)
 
     def in_views(t, rank):
         cols = pl.ds(pl.multiple_of(rank * COLS, COLS), COLS)
@@ -209,6 +213,7 @@
 
     for t in (0, 1, 2, 3):
         await_bytes(in_bufs[t], in_recv.at[t])
+    gate_load.wait()
     first_slot = x * GROUP
 
     def media_row(i):
@@ -216,7 +221,7 @@
         return jnp.where(pair >= 0, pair - first_slot, -1)
 
     def cross_step(head, c):
-        gate_row = gate_ref[pl.ds(me * HEADS + head, 1), :]
+        gate_row = gate_buf[pl.ds(me * HEADS + head, 1), :]
         gate_own[pl.ds(head, 1), :] = cross_head(
             head, gate_row, media_row, qc_buf, cot_buf, lat_buf, mixed, gqc_buf, glat_buf, acc_k, acc_v
         )
@@ -225,16 +230,15 @@
 
     lax.fori_loop(0, HEADS, cross_step, 0)
 
-    gate_x[x] = gate_own[...]
-
-    def send_x(k, c):
+    gate_all[me] = gate_own[...]
+    first = {"seq": x * GROUP}
+
+    @pl.when(jnp.logical_not(leads))
+    def _():
         pltpu.make_async_remote_copy(
-            src_ref=gate_own, dst_ref=gate_x.at[x], send_sem=gx_send.at[k], recv_sem=gx_recv.at[k],
-            device_id=along_x(k), device_id_type=MESH,
+            src_ref=gate_own, dst_ref=gate_all.at[me], send_sem=gate_send.at[stages], recv_sem=gather_recv.at[me],
+            device_id=first, device_id_type=MESH,
         ).start()
-        return c
-
-    lax.fori_loop(1, x_count, send_x, 0)
 
     for t in (4, 5, 6):
         await_bytes(in_bufs[t], in_recv.at[t])
@@ -246,54 +250,46 @@
 
     lax.fori_loop(0, HEADS, self_step, 0)
 
-    def wait_x(k, c):
-        pltpu.make_async_remote_copy(
-            src_ref=gate_own, dst_ref=gate_x.at[x], send_sem=gx_send.at[k], recv_sem=gx_recv.at[k],
-            device_id=along_x(k), device_id_type=MESH,
-        ).wait()
-        return c
-
-    lax.fori_loop(1, x_count, wait_x, 0)
-    gate_own[...] = jnp.sum(gate_x[...], axis=0)
-    gate_z[doc] = gate_own[...]
-
-    def copy_z(k):
-        return pltpu.make_async_remote_copy(
-            src_ref=gate_own, dst_ref=gate_z.at[doc], send_sem=gz_send.at[k], recv_sem=gz_recv.at[k],
-            device_id=along_z(k), device_id_type=MESH,
-        )
-
-    def send_z(k, c):
-        copy_z(k).start()
-        return c
-
-    def wait_z(k, c):
-        copy_z(k).wait()
-        return c
-
-    lax.fori_loop(1, z_count, send_z, 0)
-    lax.fori_loop(1, z_count, wait_z, 0)
-    gate_own[...] = jnp.sum(gate_z[...], axis=0)
-    gate_all[me] = gate_own[...]
-
-    def copy_group(k):
-        return pltpu.make_async_remote_copy(
-            src_ref=gate_own, dst_ref=gate_all.at[me], send_sem=gg_send.at[k], recv_sem=gg_recv.at[k],
-            device_id=in_group(k)[1], device_id_type=MESH,
-        )
-
-    def send_group(k, c):
-        copy_group(k).start()
-        return c
-
-    def wait_group(k, c):
-        copy_group(k).wait()
-        return c
-
-    lax.fori_loop(1, GROUP, send_group, 0)
-    lax.fori_loop(1, GROUP, wait_group, 0)
+    @pl.when(leads)
+    def _():
+        def gathered(rank, c):
+            await_bytes(gate_all.at[rank], gather_recv.at[rank])
+            return c
+
+        lax.fori_loop(1, GROUP, gathered, 0)
+        gate_sums[0] = gate_all[...]
+        for stage in range(stages):
+            copy = pltpu.make_async_remote_copy(
+                src_ref=gate_sums.at[stage], dst_ref=gate_in.at[stage],
+                send_sem=gate_send.at[stage], recv_sem=gate_recv.at[stage],
+                device_id=partner(stage), device_id_type=MESH,
+            )
+            copy.start()
+            copy.wait()
+            gate_sums[stage + 1] = gate_sums[stage] + gate_in[stage]
+
+        def spread(k, c):
+            pltpu.make_async_remote_copy(
+                src_ref=gate_sums.at[stages], dst_ref=gate_sums.at[stages],
+                send_sem=spread_send.at[k], recv_sem=gate_recv.at[stages],
+                device_id={"seq": x * GROUP + k}, device_id_type=MESH,
+            ).start()
+            return c
+
+        def spread_end(k, c):
+            await_bytes(gate_sums.at[stages], spread_send.at[k])
+            return c
+
+        lax.fori_loop(1, GROUP, spread, 0)
+        lax.fori_loop(1, GROUP, spread_end, 0)
+
+    @pl.when(jnp.logical_not(leads))
+    def _():
+        await_bytes(gate_own, gate_send.at[stages])
+        await_bytes(gate_sums.at[stages], gate_recv.at[stages])
+
     for rank in range(GROUP):
-        gate_out_ref[pl.ds(rank * HEADS, HEADS), :] = gate_all[rank, pl.ds(0, HEADS), :]
+        gate_out_ref[pl.ds(rank * HEADS, HEADS), :] = gate_sums[stages, rank, pl.ds(0, HEADS), :]
 
     most = GROUP - 1
     for t, buf in enumerate(in_bufs):
@@ -322,41 +318,44 @@
 
 
 def per_device(x_count, z_count, q, k, v, qc, lat, media, gate, cot):
-    any_space = pl.BlockSpec(memory_space=pl.ANY)
+    hbm = pl.BlockSpec(memory_space=pl.ANY)
     vmem = pl.BlockSpec(memory_space=pltpu.VMEM)
     token = jax.ShapeDtypeStruct((1, ROWS, WIDTH), BF16)
-    outs = (token,) * 5 + (jax.ShapeDtypeStruct(lat.shape, BF16),)
+    gate_shape = (GROUP * HEADS, E)
+    stages = (x_count * z_count).bit_length() - 1
+    outs = (token,) * 5 + (jax.ShapeDtypeStruct(lat.shape, BF16), jax.ShapeDtypeStruct(gate_shape, F32))
     tokens = pltpu.VMEM((DOC, COLS), BF16)
     latents = pltpu.VMEM((GROUP, 2, LAT, COLS), BF16)
     dma = pltpu.SemaphoreType.DMA
     results = pl.pallas_call(
         functools.partial(kernel, x_count, z_count),
         name="attention",
-        out_shape=outs + (jax.ShapeDtypeStruct((GROUP * HEADS, E), F32),),
-        in_specs=[any_space] * 7 + [vmem],
-        out_specs=[any_space] * 6 + [vmem],
+        out_shape=outs,
+        in_specs=[hbm] * 8,
+        out_specs=[hbm] * 6 + [vmem],
         scratch_shapes=[
             tokens, tokens, tokens, tokens, tokens, latents, pltpu.VMEM((GROUP, 1, ROWS), jnp.int32),
             tokens, tokens, tokens, tokens, tokens, latents,
             pltpu.VMEM((DOC, COLS), F32), pltpu.VMEM((DOC, E), F32), pltpu.VMEM((DOC, E), F32),
-            pltpu.VMEM((8, E), F32), pltpu.VMEM((x_count, 8, E), F32),
-            pltpu.VMEM((z_count, 8, E), F32), pltpu.VMEM((GROUP, 8, E), F32),
-            dma((7,)), dma((7,)), dma((6, HEADS)), dma((6, HEADS)),
-            dma((x_count,)), dma((x_count,)), dma((z_count,)), dma((z_count,)), dma((GROUP,)), dma((GROUP,)),
+            pltpu.VMEM(gate_shape, F32), pltpu.VMEM((8, E), F32), pltpu.VMEM((GROUP, 8, E), F32),
+            pltpu.VMEM((stages + 1, GROUP, 8, E), F32), pltpu.VMEM((stages, GROUP, 8, E), F32),
+            dma(()), dma((7,)), dma((7,)), dma((6, HEADS)), dma((6, HEADS)),
+            dma((GROUP,)), dma((stages + 1,)), dma((stages + 1,)), dma((GROUP,)),
         ],
         compiler_params=pltpu.CompilerParams(
-            collective_id=0, has_side_effects=True, vmem_limit_bytes=48 << 20
+            collective_id=0, has_side_effects=True, vmem_limit_bytes=47 << 20
         ),
-    )(q, k, v, qc, lat, cot, media, gate.reshape(GROUP * HEADS, E))
+    )(q, k, v, qc, lat, cot, media, gate.reshape(gate_shape))
     done = pl.pallas_call(
         finish_kernel,
         name="finish",
         out_shape=outs,
-        in_specs=[any_space] * 6,
-        out_specs=[any_space] * 6,
-        scratch_shapes=[dma((6,))],
-    )(*results[:6])
-    return (*done, results[6].reshape(WIDTH))
+        in_specs=[vmem] * 7,
+        out_specs=[hbm] * 7,
+        scratch_shapes=[dma((7,))],
+        compiler_params=pltpu.CompilerParams(vmem_limit_bytes=47 << 20),
+    )(*results)
+    return (*done[:6], done[6].reshape(WIDTH))
 
 
 def solution(mesh):

time: 348 us -> 148 us (0.43)
  Pallas kernels: 340 us -> 146 us
  local copies, waits for them, and re-layouts: 6.93 us -> 1.37 us
    pallas_call x1, Pallas kernels: 192 us -> 2.73 us  [per_device(): pl.pallas_call(finish_kernel, name='finish', out_shape=outs, in_specs=[vm...]
    unnamed x15 -> x4, local copies, waits for them, and re-layouts: 6.93 us -> 1.37 us
    pallas_call x1, Pallas kernels: 149 us -> 143 us  [per_device(): pl.pallas_call(functools.partial(kernel, x_count, z_count), name='attenti...]
where the time goes in v2:
time: 148 us
  Pallas kernels  146 us (99%)
    pallas_call x1, Pallas kernels, per_device(): pl.pallas_call(functools.partial(kernel, x_count, z_count), name='attenti...  143 us

profile of v2, /device:TPU:1, one launch (start us, length us, event | category | flops | bytes accessed | tf_op | source)
XLA Modules:
  0.0 148.2 jit_solution(17382885689425739299)
XLA Ops:
  0.6 0.0 copy-start.1
  0.6 0.6 copy-done.1
  1.3 0.0 copy-start
  1.3 0.7 copy-done
  2.0 143.5 %attention.1 = (bf16[1,128,4096]{2,1,0:T(8,128)(2,1)S(1)}, bf16[1,128,4096]{2,1,0:T(8,128)(2,1)S(1)}, bf16[1,128,4096]{2,1,0:T(8,128)(2,1)S(1)}, bf16[1,128,4096...) custom-call(bf16[1,128,4096]{2,1,0:T(8,128)(2,1)} %q_ref.1, ...), custom_call_target="tpu_custom_call" | custom-call | tf_op jit(solution)/shard_map/attention/pallas_call | solution.py:330
  145.5 2.7 %finish.1 = (bf16[1,128,4096]{2,1,0:T(8,128)(2,1)}, bf16[1,128,4096]{2,1,0:T(8,128)(2,1)}, bf16[1,128,4096]{2,1,0:T(8,128)(2,1)}, bf16[1,128,4096]{2,1,0:T(8,128...) custom-call(bf16[1,128,4096]{2,1,0:T(8,128)(2,1)S(1)} %get-tuple-element.21.refs_0_, ...), custom_call_target="tpu_custom_call" | custom-call | tf_op jit(solution)/shard_map/finish/pallas_call | solution.py:349
Async XLA Ops:
  0.6 0.7 copy-start.1
  1.3 0.7 copy-start

commit v3 on v2

v3 whole, which is shorter than its diff:
```python
import functools

import jax
import jax.numpy as jnp
from jax import lax
from jax.experimental import pallas as pl
from jax.experimental.pallas import tpu as pltpu
from jax.sharding import PartitionSpec as P

E = 128
LAT = 64
GROUP = 8
ROWS = 128
BLOCK = 256
DOC = GROUP * ROWS
KEYS = GROUP * LAT
A, B = 0, 1
HEADS = (5, 3)
BATCHES = (((0, 2), (2, 3)), ((0, 3),))
HERE = (0, 5)
THERE = (0, 20)
ALL_HEADS = 32
WIDTH = ALL_HEADS * E
COLS = sum(HEADS) * E
SCALE = E**-0.5
NEG_FILL = -1e30
MESH = pl.DeviceIdType.MESH
F32 = jnp.float32
BF16 = jnp.bfloat16


def dot(left, right, left_dim, right_dim):
    return lax.dot_general(
        left, right, (((left_dim,), (right_dim,)), ((), ())), preferred_element_type=F32
    )


def softmax_and_grad(scores, weights_grad_of, inverse_of):
    peak = jnp.max(scores, axis=0, keepdims=True)
    weights = jnp.exp(SCALE * (scores - peak))
    weights = weights * inverse_of(jnp.sum(weights, axis=0, keepdims=True))
    half = weights.astype(BF16)
    weights_grad = weights_grad_of()
    inner = jnp.sum(weights * weights_grad, axis=0, keepdims=True)
    return half, (weights * (weights_grad - inner)).astype(BF16)


def head_cols(job, head):
    return pl.ds(pl.multiple_of((HERE[job] + head) * E, E), E)


def cross_head(cols, gate_row, media_row, qc_buf, cot_buf, lat_buf, mixed, gqc_buf, glat_buf):
    keys = lat_buf[:, 0, :, cols].reshape(KEYS, E)
    values = lat_buf[:, 1, :, cols].reshape(KEYS, E)
    tanh_gate = jnp.tanh(gate_row)
    slot = lax.broadcasted_iota(jnp.int32, (KEYS, BLOCK), 0) // LAT
    gate_sum = jnp.zeros((1, E), F32)
    keys_grad = jnp.zeros((KEYS, E), F32)
    values_grad = jnp.zeros((KEYS, E), F32)
    for i in range(2):
        rows = pl.ds(i * BLOCK, BLOCK)
        cited = media_row(i)
        queries = qc_buf[rows, cols]
        cot = cot_buf[rows, cols].astype(F32)
        cot_cross = (cot * tanh_gate).astype(BF16)
        scores = dot(keys, queries, 1, 1)
        scores = jnp.where(slot == cited, scores, NEG_FILL)
        half, scores_grad = softmax_and_grad(
            scores,
            lambda: dot(values, cot_cross, 1, 1),
            lambda total: jnp.where(cited >= 0, 1.0 / total, 0.0),
        )
        out = dot(values, half, 0, 0).T
        mixed[rows, cols] = tanh_gate * out
        values_grad += dot(half, cot_cross, 1, 0)
        gqc_buf[rows, cols] = (SCALE * dot(keys, scores_grad, 0, 0)).T.astype(BF16)
        keys_grad += dot(scores_grad, queries, 1, 0)
        gate_sum += jnp.sum(cot * out, axis=0, keepdims=True)
    glat_buf[:, 0, :, cols] = (SCALE * keys_grad).astype(BF16).reshape(GROUP, LAT, E)
    glat_buf[:, 1, :, cols] = values_grad.astype(BF16).reshape(GROUP, LAT, E)
    return gate_sum * (1.0 - tanh_gate * tanh_gate)


def self_block(i, place, cols, q_buf, k_buf, v_buf, cot_buf, mixed, out_buf, gq_buf, acc_k, acc_v):
    rows = pl.ds(place * BLOCK, BLOCK)
    seen = pl.ds(0, (i + 1) * BLOCK)
    queries = q_buf[rows, cols]
    cot = cot_buf[rows, cols]
    keys = k_buf[seen, cols]
    values = v_buf[seen, cols]
    scores = dot(keys, queries, 1, 1)
    shape = scores.shape
    causal = lax.broadcasted_iota(jnp.int32, shape, 0) <= i * BLOCK + lax.broadcasted_iota(jnp.int32, shape, 1)
    scores = jnp.where(causal, scores, -jnp.inf)
    half, scores_grad = softmax_and_grad(
        scores, lambda: dot(values, cot, 1, 1), lambda total: 1.0 / total
    )
    out = dot(values, half, 0, 0).T
    out_buf[rows, cols] = (out + mixed[rows, cols]).astype(BF16)
    acc_v[seen, :] += dot(half, cot, 1, 0)
    gq_buf[rows, cols] = (SCALE * dot(keys, scores_grad, 0, 0)).T.astype(BF16)
    acc_k[seen, :] += dot(scores_grad, queries, 1, 0)


def kernel(
    x_count, z_count,
    q_ref, k_ref, v_ref, qc_ref, lat_ref, cot_ref, media_ref, gate_ref,
    out_ref, gq_ref, gk_ref, gv_ref, gqc_ref, glat_ref, gate_out_ref,
    q_buf, qc_buf, cot_buf, k_buf, v_buf, lat_buf, media_buf,
    out_buf, gq_buf, gqc_buf, gk_buf, gv_buf, glat_buf, gk_in, gv_in, glat_in,
    mixed, acc_k, acc_v, gate_buf, gate_own, gate_all, gate_sums, gate_in,
    gate_sem, media_send, media_recv, in_send, in_recv, pass_send, pass_recv, part_send, part_recv,
    out_send, out_recv, gather_recv, gate_send, gate_recv, spread_send,
):
    seq = lax.axis_index("seq")
    doc = lax.axis_index("doc")
    x = seq // GROUP
    me = lax.rem(seq, GROUP)
    chip = me // 2
    core = lax.rem(me, 2)
    mirror = 3 - chip
    pair = chip + 1 - 2 * lax.rem(chip, 2)
    homes = ((chip, mirror), (chip, pair))
    partner = (pair, mirror)
    inner = lax.rem((chip + 1) // 2, 2)
    low = chip < 2
    is_inner = inner == 1
    not_ = jnp.logical_not

    def at(chip, core):
        return {"seq": x * GROUP + chip * 2 + core}

    def in_group(k):
        rank = lax.rem(me + k, GROUP)
        return rank, {"seq": x * GROUP + rank}

    leads = me == 0
    group_at = x + x_count * doc
    stages = (x_count * z_count).bit_length() - 1

    def gate_partner(stage):
        bit = 1 << stage
        other = group_at + bit - 2 * bit * lax.rem(group_at // bit, 2)
        return {"seq": lax.rem(other, x_count) * GROUP, "doc": other // x_count}

    barrier = pltpu.get_barrier_semaphore()

    def greet(device):
        pl.semaphore_signal(barrier, inc=1, device_id=device, device_id_type=MESH)

    def greet_group(k, c):
        greet(in_group(k)[1])
        return c

    lax.fori_loop(1, GROUP, greet_group, 0)

    @pl.when(leads)
    def _():
        for stage in range(stages):
            greet(gate_partner(stage))
        pl.semaphore_wait(barrier, GROUP - 1 + stages)

    @pl.when(not_(leads))
    def _():
        pl.semaphore_wait(barrier, GROUP - 1)

    def send(src, dst, send_sem, recv_sem, device):
        pltpu.make_async_remote_copy(
            src_ref=src, dst_ref=dst, send_sem=send_sem, recv_sem=recv_sem,
            device_id=device, device_id_type=MESH,
        ).start()

    def await_bytes(ref, sem):
        pltpu.make_async_copy(ref, ref, sem).wait()

    def here(job):
        return pl.ds(HERE[job] * E, HEADS[job] * E)

    def first_head(job, chip, core):
        plan = chip // 2 if job == A else lax.rem((chip + 1) // 2, 2)
        return THERE[job] + (plan * 2 + core) * HEADS[job]

    def there(job, chip, core):
        return pl.ds(pl.multiple_of(first_head(job, chip, core) * E, E), HEADS[job] * E)

    def place(job, chip):
        return chip // 2 if job == A else lax.rem(chip, 2)

    def rows_at(block, core):
        return pl.ds(pl.multiple_of(block * BLOCK + core * ROWS, ROWS), ROWS)

    gate_load = pltpu.make_async_copy(gate_ref, gate_buf, gate_sem)
    gate_load.start()
    pltpu.make_async_copy(media_ref, media_buf.at[me], media_recv).start()

    def send_media(k, c):
        send(media_ref, media_buf.at[me], media_send, media_recv, in_group(k)[1])
        return c

    lax.fori_loop(1, GROUP, send_media, 0)

    K, V, LATS, COT, QC, Q = range(6)
    refs = (k_ref, v_ref, lat_ref, cot_ref, qc_ref, q_ref)
    bufs = (k_buf, v_buf, lat_buf, cot_buf, qc_buf, q_buf)

    def in_views(t, job, to_chip, to_core):
        cols = there(job, to_chip, to_core)
        if t == LATS:
            return lat_ref.at[0, 0, :, :, cols], lat_buf.at[me, :, :, here(job)]
        rows = rows_at(chip, core) if t in (K, V) else rows_at(place(job, chip), core)
        return refs[t].at[0, :, cols], bufs[t].at[rows, here(job)]

    def send_in(t, job):
        src, dst = in_views(t, job, chip, core)
        pltpu.make_async_copy(src, dst, in_recv.at[job, t]).start()
        for to_chip, to_core in ((homes[job][1], core), (homes[job][1], 1 - core), (chip, 1 - core)):
            src, dst = in_views(t, job, to_chip, to_core)
            send(src, dst, in_send.at[job, t], in_recv.at[job, t], at(to_chip, to_core))

    for t in (LATS, K, V, COT, QC, Q):
        send_in(t, A)
        if t != Q:
            send_in(t, B)

    def await_in(t, job):
        if t == LATS:
            await_bytes(lat_buf.at[pl.ds(0, 4), :, :, here(job)], in_recv.at[job, t])
        else:
            await_bytes(q_buf.at[:, here(job)], in_recv.at[job, t])

    def pass_on(job, t, first, count):
        part = bufs[t].at[pl.ds(first, count), :, :, here(job)] if t == LATS else bufs[t].at[pl.ds(first, count), here(job)]
        send(part, part, pass_send.at[job, t], pass_recv.at[job, t], at(partner[job], core))

    for job in (A, B):
        await_in(LATS, job)
    pl.when(not_(is_inner))(lambda: (pass_on(A, LATS, 0, 2), pass_on(A, LATS, 6, 2)) and None)
    pl.when(is_inner)(lambda: pass_on(A, LATS, 2, 4))
    pl.when(low)(lambda: pass_on(B, LATS, 0, 4))
    pl.when(not_(low))(lambda: pass_on(B, LATS, 4, 4))
    for t in (K, V):
        for job in (A, B):
            await_in(t, job)
        pl.when(not_(is_inner))(lambda: pass_on(A, t, 0, BLOCK))
        pl.when(is_inner)(lambda: pass_on(A, t, BLOCK, 2 * BLOCK))
        pl.when(low)(lambda: pass_on(B, t, 0, 2 * BLOCK))
    send_in(Q, B)

    OUT, GQ, GQC, GK, GV, GLAT = range(6)
    out_refs = (out_ref, gq_ref, gqc_ref, gk_ref, gv_ref, glat_ref)
    out_bufs = (out_buf, gq_buf, gqc_buf, gk_buf, gv_buf, glat_buf)

    def out_views(t, job, to_chip, to_core, first, count):
        near = pl.ds((HERE[job] + first) * E, count * E)
        far = pl.ds(pl.multiple_of((first_head(job, chip, core) + first) * E, E), count * E)
        if t == GLAT:
            return glat_buf.at[to_chip * 2 + to_core, :, :, near], glat_ref.at[0, 0, :, :, far]
        rows = rows_at(to_chip, to_core) if t in (GK, GV) else rows_at(place(job, to_chip), to_core)
        return out_bufs[t].at[rows, near], out_refs[t].at[0, :, far]

    def send_home(job, part, first=0, count=None):
        count = count or HEADS[job]
        for t in part:
            src, dst = out_views(t, job, chip, core, first, count)
            pltpu.make_async_copy(src, dst, out_recv.at[t]).start()
            for to_chip, to_core in ((homes[job][1], core), (homes[job][1], 1 - core), (chip, 1 - core)):
                src, dst = out_views(t, job, to_chip, to_core, first, count)
                send(src, dst, out_send.at[job, t], out_recv.at[t], at(to_chip, to_core))

    await_bytes(media_buf, media_recv)
    gate_load.wait()
    first_slot = x * GROUP

    def send_glat(job, first, count):
        send(
            glat_buf.at[pl.ds(first, count), :, :, here(job)], glat_in.at[pl.ds(first, count), :, :, here(job)],
            part_send.at[job, 2], part_recv.at[job, 2], at(partner[job], core),
        )

    for job in (A, B):
        await_in(COT, job)
        await_in(QC, job)
        await_bytes(lat_buf.at[pl.ds(0, 4), :, :, here(job)], pass_recv.at[job, LATS])
        head_of = first_head(job, chip, core)

        def media_row(i, job=job):
            block = (3 * i * (1 - inner) + (1 + i) * inner) if job == A else 2 * (chip // 2) + i
            cited = jnp.concatenate([media_buf[2 * block], media_buf[2 * block + 1]], axis=1)
            return jnp.where(cited >= 0, cited - first_slot, -1)

        def cross_step(head, c, job=job, head_of=head_of, media_row=media_row):
            gate_own[pl.ds(HERE[job] + head, 1), :] = cross_head(
                head_cols(job, head), gate_buf[pl.ds(head_of + head, 1), :], media_row,
                qc_buf, cot_buf, lat_buf, mixed, gqc_buf, glat_buf,
            )
            return c

        lax.fori_loop(0, HEADS[job], cross_step, 0)
        if job == B:
            gate_all[me] = gate_own[...]

            @pl.when(not_(leads))
            def _():
                send(gate_own, gate_all.at[me], gate_send.at[stages], gather_recv.at[me], {"seq": x * GROUP})

        if job == A:
            pl.when(not_(is_inner))(lambda: send_glat(A, 2, 4))
            pl.when(is_inner)(lambda: (send_glat(A, 0, 2), send_glat(A, 6, 2)) and None)
        else:
            pl.when(low)(lambda: send_glat(B, 4, 4))
            pl.when(not_(low))(lambda: send_glat(B, 0, 4))
        send_home(job, (GQC,))

    def send_part(job, first_row, row_count, first, count):
        rows, cols = pl.ds(first_row, row_count), pl.ds((HERE[job] + first) * E, count * E)
        for t, (buf, into) in enumerate(((gk_buf, gk_in), (gv_buf, gv_in))):
            send(buf.at[rows, cols], into.at[rows, cols], part_send.at[job, t], part_recv.at[job, t], at(partner[job], core))

    for job in (A, B):
        await_in(Q, job)
        for t in (K, V):
            if job == A:
                pl.when(not_(is_inner))(lambda: await_bytes(k_buf.at[pl.ds(0, 2 * BLOCK), here(A)], pass_recv.at[A, t]))
                pl.when(is_inner)(lambda: await_bytes(k_buf.at[pl.ds(0, BLOCK), here(A)], pass_recv.at[A, t]))
            else:
                pl.when(not_(low))(lambda: await_bytes(k_buf.at[pl.ds(0, 2 * BLOCK), here(B)], pass_recv.at[B, t]))

        def self_step(head, c, job=job):
            cols = head_cols(job, head)
            acc_k[...] = jnp.zeros((DOC, E), F32)
            acc_v[...] = jnp.zeros((DOC, E), F32)

            def block(i):
                self_block(
                    i, place(job, i) if job == A else i % 2, cols,
                    q_buf, k_buf, v_buf, cot_buf, mixed, out_buf, gq_buf, acc_k, acc_v,
                )

            if job == A:
                pl.when(not_(is_inner))(lambda: (block(0), block(3)) and None)
                pl.when(is_inner)(lambda: (block(1), block(2)) and None)
            else:
                pl.when(low)(lambda: (block(0), block(1)) and None)
                pl.when(not_(low))(lambda: (block(2), block(3)) and None)
            gk_buf[:, cols] = (SCALE * acc_k[...]).astype(BF16)
            gv_buf[:, cols] = acc_v[...].astype(BF16)
            for first, count in BATCHES[job]:

                @pl.when(head == first + count - 1)
                def _(first=first, count=count):
                    if job == A:
                        pl.when(not_(is_inner))(lambda: send_part(A, BLOCK, 2 * BLOCK, first, count))
                        pl.when(is_inner)(lambda: send_part(A, 0, BLOCK, first, count))
                    else:
                        pl.when(not_(low))(lambda: send_part(B, 0, 2 * BLOCK, first, count))
                    send_home(job, (OUT, GQ), first, count)

            return c

        lax.fori_loop(0, HEADS[job], self_step, 0)

    def add(buf, into, *where):
        buf[where] = (buf[where].astype(F32) + into[where].astype(F32)).astype(BF16)

    def add_glat(job, first, count):
        add(glat_buf, glat_in, pl.ds(first, count), slice(None), slice(None), here(job))

    def add_part(job, t, first, count):
        buf, into = ((gk_buf, gk_in), (gv_buf, gv_in))[t]
        await_bytes(into.at[pl.ds(first, count), here(job)], part_recv.at[job, t])
        add(buf, into, pl.ds(first, count), here(job))

    def finish_glat(job):
        await_bytes(glat_in.at[pl.ds(0, 4), :, :, here(job)], part_recv.at[job, 2])
        if job == A:
            pl.when(not_(is_inner))(lambda: (add_glat(A, 0, 2), add_glat(A, 6, 2)) and None)
            pl.when(is_inner)(lambda: add_glat(A, 2, 4))
        else:
            pl.when(low)(lambda: add_glat(B, 0, 4))
            pl.when(not_(low))(lambda: add_glat(B, 4, 4))
        send_home(job, (GLAT,))

    def finish_part(job):
        for t, result in enumerate((GK, GV)):
            if job == A:
                pl.when(not_(is_inner))(lambda: add_part(A, t, 0, BLOCK))
                pl.when(is_inner)(lambda: add_part(A, t, BLOCK, 2 * BLOCK))
            else:
                pl.when(low)(lambda: add_part(B, t, 0, 2 * BLOCK))
            send_home(job, (result,))

    def gate_copy(stage):
        return pltpu.make_async_remote_copy(
            src_ref=gate_sums.at[stage], dst_ref=gate_in.at[stage],
            send_sem=gate_send.at[stage], recv_sem=gate_recv.at[stage],
            device_id=gate_partner(stage), device_id_type=MESH,
        )

    def gate_stage(stage):
        @pl.when(leads)
        def _():
            if stage == 0:
                def gathered(rank, c):
                    await_bytes(gate_all.at[rank], gather_recv.at[rank])
                    return c

                lax.fori_loop(1, GROUP, gathered, 0)
                gate_sums[0] = gate_all[...]
            else:
                gate_copy(stage - 1).wait()
                gate_sums[stage] = gate_sums[stage - 1] + gate_in[stage - 1]
            if stage < stages:
                gate_copy(stage).start()
            else:
                def spread(k, c):
                    send(
                        gate_sums.at[stages], gate_sums.at[stages], spread_send.at[k], gate_recv.at[stages],
                        {"seq": x * GROUP + k},
                    )
                    return c

                lax.fori_loop(1, GROUP, spread, 0)

    gate_stage(0)
    finish_glat(A)
    gate_stage(1)
    finish_glat(B)
    gate_stage(2)
    finish_part(B)
    for stage in range(3, stages):
        gate_stage(stage)
    finish_part(A)
    gate_stage(stages)

    @pl.when(leads)
    def _():
        def spread_end(k, c):
            await_bytes(gate_sums.at[stages], spread_send.at[k])
            return c

        lax.fori_loop(1, GROUP, spread_end, 0)

    @pl.when(not_(leads))
    def _():
        await_bytes(gate_own, gate_send.at[stages])
        await_bytes(gate_sums.at[stages], gate_recv.at[stages])

    for job, owners in ((A, ((0, 1), (2, 3))), (B, ((0, 3), (1, 2)))):
        part = pl.ds(HERE[job], HEADS[job])
        for plan, (one, two) in enumerate(owners):
            for side in range(2):
                first = THERE[job] + (plan * 2 + side) * HEADS[job]
                gate_out_ref[pl.ds(first, HEADS[job]), :] = (
                    gate_sums[stages, one * 2 + side, part, :] + gate_sums[stages, two * 2 + side, part, :]
                )

    await_bytes(media_buf.at[pl.ds(0, GROUP - 1)], media_send)
    for job in (A, B):
        for t in range(6):
            sent = lat_buf.at[pl.ds(0, 3), :, :, here(job)] if t == LATS else q_buf.at[pl.ds(0, 3 * ROWS), here(job)]
            await_bytes(sent, in_send.at[job, t])
            sent = glat_buf.at[pl.ds(0, 3), :, :, here(job)] if t == GLAT else out_buf.at[pl.ds(0, 3 * ROWS), here(job)]
            await_bytes(sent, out_send.at[job, t])
        await_bytes(lat_buf.at[pl.ds(0, 4), :, :, here(job)], pass_send.at[job, LATS])
        await_bytes(glat_buf.at[pl.ds(0, 4), :, :, here(job)], part_send.at[job, 2])

    def sent_rows(job, rows, pass_only, part_only):
        for t in (0, 1):
            if pass_only:
                await_bytes(k_buf.at[pl.ds(0, rows), here(job)], pass_send.at[job, t])
            if part_only:
                await_bytes(gk_buf.at[pl.ds(0, rows), here(job)], part_send.at[job, t])

    @pl.when(is_inner)
    def _():
        sent_rows(A, 2 * BLOCK, True, False)
        sent_rows(A, BLOCK, False, True)

    @pl.when(not_(is_inner))
    def _():
        sent_rows(A, BLOCK, True, False)
        sent_rows(A, 2 * BLOCK, False, True)

    pl.when(low)(lambda: sent_rows(B, 2 * BLOCK, True, False))
    pl.when(not_(low))(lambda: sent_rows(B, 2 * BLOCK, False, True))
    for t in range(6):
        await_bytes(out_refs[t], out_recv.at[t])


def finish_kernel(*refs):
    count = len(refs) // 2
    sems = refs[-1]
    copies = [pltpu.make_async_copy(refs[i], refs[count + i], sems.at[i]) for i in range(count)]
    for copy in copies:
        copy.start()
    for copy in copies:
        copy.wait()


def per_device(x_count, z_count, q, k, v, qc, lat, media, gate, cot):
    anywhere = pl.BlockSpec(memory_space=pl.ANY)
    vmem = pl.BlockSpec(memory_space=pltpu.VMEM)
    token = jax.ShapeDtypeStruct((1, ROWS, WIDTH), BF16)
    gate_shape = (ALL_HEADS, E)
    stages = (x_count * z_count).bit_length() - 1
    outs = (token,) * 5 + (jax.ShapeDtypeStruct(lat.shape, BF16), jax.ShapeDtypeStruct(gate_shape, F32))
    queries = pltpu.VMEM((2 * BLOCK, COLS), BF16)
    tokens = pltpu.VMEM((DOC, COLS), BF16)
    latents = pltpu.VMEM((GROUP, 2, LAT, COLS), BF16)
    dma = pltpu.SemaphoreType.DMA
    results = pl.pallas_call(
        functools.partial(kernel, x_count, z_count),
        name="attention",
        out_shape=outs,
        in_specs=[anywhere] * 8,
        out_specs=[anywhere] * 6 + [vmem],
        scratch_shapes=[
            queries, queries, queries, tokens, tokens, latents, pltpu.VMEM((GROUP, 1, ROWS), jnp.int32),
            queries, queries, queries, tokens, tokens, latents, tokens, tokens, latents,
            pltpu.VMEM((2 * BLOCK, COLS), F32), pltpu.VMEM((DOC, E), F32), pltpu.VMEM((DOC, E), F32),
            pltpu.VMEM(gate_shape, F32), pltpu.VMEM((8, E), F32), pltpu.VMEM((GROUP, 8, E), F32),
            pltpu.VMEM((stages + 1, GROUP, 8, E), F32), pltpu.VMEM((stages, GROUP, 8, E), F32),
            dma(()), dma(()), dma(()), dma((2, 6)), dma((2, 6)), dma((2, 3)), dma((2, 3)), dma((2, 3)), dma((2, 3)),
            dma((2, 6)), dma((6,)), dma((GROUP,)), dma((stages + 1,)), dma((stages + 1,)), dma((GROUP,)),
        ],
        compiler_params=pltpu.CompilerParams(
            collective_id=0, has_side_effects=True, vmem_limit_bytes=95 << 19
        ),
    )(q, k, v, qc, lat, cot, media, gate.reshape(gate_shape))
    done = pl.pallas_call(
        finish_kernel,
        name="finish",
        out_shape=outs,
        in_specs=[vmem] * 7,
        out_specs=[anywhere] * 7,
        scratch_shapes=[dma((7,))],
        compiler_params=pltpu.CompilerParams(vmem_limit_bytes=47 << 20),
    )(*results)
    return (*done[:6], done[6].reshape(WIDTH))


def solution(mesh):
    token = P("doc", "seq", None)
    latent = P("doc", "seq", None, None, None)
    return jax.shard_map(
        functools.partial(per_device, mesh.shape["seq"] // GROUP, mesh.shape["doc"]),
        mesh=mesh,
        in_specs=(token, token, token, token, latent, P("doc", "seq"), P(), token),
        out_specs=(token, token, token, token, token, latent, P()),
        check_vma=False,
    )
```

time: 148 us -> 135 us (0.912)
  Pallas kernels: 146 us -> 133 us
    pallas_call x1, Pallas kernels: 143 us -> 130 us  [per_device(): pl.pallas_call(functools.partial(kernel, x_count, z_count), name='attenti...]
where the time goes in v3:
time: 135 us
  Pallas kernels  133 us (99%)
  local copies, waits for them, and re-layouts  1.37 us (1%)
    pallas_call x1, Pallas kernels, per_device(): pl.pallas_call(functools.partial(kernel, x_count, z_count), name='attenti...  130 us
    pallas_call x1, Pallas kernels, per_device(): pl.pallas_call(finish_kernel, name='finish', out_shape=outs, in_specs=[vm...  2.73 us

profile of v3, /device:TPU:1, one launch (start us, length us, event | category | flops | bytes accessed | tf_op | source)
XLA Modules:
  0.0 134.5 jit_solution(14657350694037169926)
XLA Ops:
  0.6 0.0 copy-start.1
  0.6 0.6 copy-done.1
  1.3 0.0 copy-start
  1.3 0.7 copy-done
  2.0 129.8 %attention.1 = (bf16[1,128,4096]{2,1,0:T(8,128)(2,1)S(1)}, bf16[1,128,4096]{2,1,0:T(8,128)(2,1)S(1)}, bf16[1,128,4096]{2,1,0:T(8,128)(2,1)S(1)}, bf16[1,128,4096...) custom-call(bf16[1,128,4096]{2,1,0:T(8,128)(2,1)} %q_ref.1, ...), custom_call_target="tpu_custom_call" | custom-call | tf_op jit(solution)/shard_map/attention/pallas_call | solution.py:511
  131.8 2.7 %finish.1 = (bf16[1,128,4096]{2,1,0:T(8,128)(2,1)}, bf16[1,128,4096]{2,1,0:T(8,128)(2,1)}, bf16[1,128,4096]{2,1,0:T(8,128)(2,1)}, bf16[1,128,4096]{2,1,0:T(8,128...) custom-call(bf16[1,128,4096]{2,1,0:T(8,128)(2,1)S(1)} %get-tuple-element.21.refs_0_, ...), custom_call_target="tpu_custom_call" | custom-call | tf_op jit(solution)/shard_map/finish/pallas_call | solution.py:530
Async XLA Ops:
  0.6 0.7 copy-start.1
  1.3 0.7 copy-start

commit v4 on v3

--- a/solution.py
+++ b/solution.py
@@ -16,7 +16,7 @@
 KEYS = GROUP * LAT
 A, B = 0, 1
 HEADS = (5, 3)
-BATCHES = (((0, 2), (2, 3)), ((0, 3),))
+BATCHES = (((0, 1), (1, 2), (3, 2)), ((0, 3),))
 HERE = (0, 5)
 THERE = (0, 20)
 ALL_HEADS = 32
@@ -158,11 +158,7 @@
     def _():
         for stage in range(stages):
             greet(gate_partner(stage))
-        pl.semaphore_wait(barrier, GROUP - 1 + stages)
-
-    @pl.when(not_(leads))
-    def _():
-        pl.semaphore_wait(barrier, GROUP - 1)
+
 
     def send(src, dst, send_sem, recv_sem, device):
         pltpu.make_async_remote_copy(
@@ -188,16 +184,6 @@
 
     def rows_at(block, core):
         return pl.ds(pl.multiple_of(block * BLOCK + core * ROWS, ROWS), ROWS)
-
-    gate_load = pltpu.make_async_copy(gate_ref, gate_buf, gate_sem)
-    gate_load.start()
-    pltpu.make_async_copy(media_ref, media_buf.at[me], media_recv).start()
-
-    def send_media(k, c):
-        send(media_ref, media_buf.at[me], media_send, media_recv, in_group(k)[1])
-        return c
-
-    lax.fori_loop(1, GROUP, send_media, 0)
 
     K, V, LATS, COT, QC, Q = range(6)
     refs = (k_ref, v_ref, lat_ref, cot_ref, qc_ref, q_ref)
@@ -210,17 +196,37 @@
         rows = rows_at(chip, core) if t in (K, V) else rows_at(place(job, chip), core)
         return refs[t].at[0, :, cols], bufs[t].at[rows, here(job)]
 
+    gate_load = pltpu.make_async_copy(gate_ref, gate_buf, gate_sem)
+    gate_load.start()
+    pltpu.make_async_copy(media_ref, media_buf.at[me], media_recv).start()
+    for t in (LATS, K, V, COT, QC, Q):
+        for job in (A, B):
+            src, dst = in_views(t, job, chip, core)
+            pltpu.make_async_copy(src, dst, in_recv.at[job, t]).start()
+
+    @pl.when(leads)
+    def _():
+        pl.semaphore_wait(barrier, GROUP - 1 + stages)
+
+    @pl.when(not_(leads))
+    def _():
+        pl.semaphore_wait(barrier, GROUP - 1)
+
     def send_in(t, job):
-        src, dst = in_views(t, job, chip, core)
-        pltpu.make_async_copy(src, dst, in_recv.at[job, t]).start()
         for to_chip, to_core in ((homes[job][1], core), (homes[job][1], 1 - core), (chip, 1 - core)):
             src, dst = in_views(t, job, to_chip, to_core)
             send(src, dst, in_send.at[job, t], in_recv.at[job, t], at(to_chip, to_core))
+
+    def send_media(k, c):
+        send(media_ref, media_buf.at[me], media_send, media_recv, in_group(k)[1])
+        return c
 
     for t in (LATS, K, V, COT, QC, Q):
         send_in(t, A)
         if t != Q:
             send_in(t, B)
+        if t == LATS:
+            lax.fori_loop(1, GROUP, send_media, 0)
 
     def await_in(t, job):
         if t == LATS:

time: 135 us -> 134 us (level)
  no operation moved by 1% of the time
where the time goes in v4:
time: 134 us
  Pallas kernels  132 us (99%)
  local copies, waits for them, and re-layouts  1.37 us (1%)
    pallas_call x1, Pallas kernels, per_device(): pl.pallas_call(functools.partial(kernel, x_count, z_count), name='attenti...  129 us
    pallas_call x1, Pallas kernels, per_device(): pl.pallas_call(finish_kernel, name='finish', out_shape=outs, in_specs=[vm...  2.73 us

profile of v4, /device:TPU:1, one launch (start us, length us, event | category | flops | bytes accessed | tf_op | source)
XLA Modules:
  0.0 133.8 jit_solution(5590790694361950394)
XLA Ops:
  0.6 0.0 copy-start.1
  0.6 0.6 copy-done.1
  1.3 0.0 copy-start
  1.3 0.7 copy-done
  2.0 129.1 %attention.1 = (bf16[1,128,4096]{2,1,0:T(8,128)(2,1)S(1)}, bf16[1,128,4096]{2,1,0:T(8,128)(2,1)S(1)}, bf16[1,128,4096]{2,1,0:T(8,128)(2,1)S(1)}, bf16[1,128,4096...) custom-call(bf16[1,128,4096]{2,1,0:T(8,128)(2,1)} %q_ref.1, ...), custom_call_target="tpu_custom_call" | custom-call | tf_op jit(solution)/shard_map/attention/pallas_call | solution.py:517
  131.1 2.7 %finish.1 = (bf16[1,128,4096]{2,1,0:T(8,128)(2,1)}, bf16[1,128,4096]{2,1,0:T(8,128)(2,1)}, bf16[1,128,4096]{2,1,0:T(8,128)(2,1)}, bf16[1,128,4096]{2,1,0:T(8,128...) custom-call(bf16[1,128,4096]{2,1,0:T(8,128)(2,1)S(1)} %get-tuple-element.21.refs_0_, ...), custom_call_target="tpu_custom_call" | custom-call | tf_op jit(solution)/shard_map/finish/pallas_call | solution.py:536
Async XLA Ops:
  0.6 0.7 copy-start.1
  1.3 0.7 copy-start

commit v5 on v4

--- a/solution.py
+++ b/solution.py
@@ -196,7 +196,7 @@
         rows = rows_at(chip, core) if t in (K, V) else rows_at(place(job, chip), core)
         return refs[t].at[0, :, cols], bufs[t].at[rows, here(job)]
 
-    gate_load = pltpu.make_async_copy(gate_ref, gate_buf, gate_sem)
+    gate_load = pltpu.make_async_copy(gate_ref, gate_buf.at[pl.ds(0, ALL_HEADS)], gate_sem)
     gate_load.start()
     pltpu.make_async_copy(media_ref, media_buf.at[me], media_recv).start()
     for t in (LATS, K, V, COT, QC, Q):
@@ -303,11 +303,11 @@
 
         lax.fori_loop(0, HEADS[job], cross_step, 0)
         if job == B:
-            gate_all[me] = gate_own[...]
+            gate_all[me] = gate_own[pl.ds(0, 8), :]
 
             @pl.when(not_(leads))
             def _():
-                send(gate_own, gate_all.at[me], gate_send.at[stages], gather_recv.at[me], {"seq": x * GROUP})
+                send(gate_own.at[pl.ds(0, 8)], gate_all.at[me], gate_send.at[stages], gather_recv.at[me], {"seq": x * GROUP})
 
         if job == A:
             pl.when(not_(is_inner))(lambda: send_glat(A, 2, 4))
@@ -448,17 +448,17 @@
 
     @pl.when(not_(leads))
     def _():
-        await_bytes(gate_own, gate_send.at[stages])
+        await_bytes(gate_own.at[pl.ds(0, 8)], gate_send.at[stages])
         await_bytes(gate_sums.at[stages], gate_recv.at[stages])
 
+    heads = []
     for job, owners in ((A, ((0, 1), (2, 3))), (B, ((0, 3), (1, 2)))):
-        part = pl.ds(HERE[job], HEADS[job])
-        for plan, (one, two) in enumerate(owners):
+        part = slice(HERE[job], HERE[job] + HEADS[job])
+        for one, two in owners:
             for side in range(2):
-                first = THERE[job] + (plan * 2 + side) * HEADS[job]
-                gate_out_ref[pl.ds(first, HEADS[job]), :] = (
-                    gate_sums[stages, one * 2 + side, part, :] + gate_sums[stages, two * 2 + side, part, :]
-                )
+                both = gate_sums[stages, one * 2 + side] + gate_sums[stages, two * 2 + side]
+                heads.append(both[part])
+    gate_out_ref[...] = jnp.concatenate(heads, axis=0)
 
     await_bytes(media_buf.at[pl.ds(0, GROUP - 1)], media_send)
     for job in (A, B):
@@ -524,7 +524,7 @@
             queries, queries, queries, tokens, tokens, latents, pltpu.VMEM((GROUP, 1, ROWS), jnp.int32),
             queries, queries, queries, tokens, tokens, latents, tokens, tokens, latents,
             pltpu.VMEM((2 * BLOCK, COLS), F32), pltpu.VMEM((DOC, E), F32), pltpu.VMEM((DOC, E), F32),
-            pltpu.VMEM(gate_shape, F32), pltpu.VMEM((8, E), F32), pltpu.VMEM((GROUP, 8, E), F32),
+            pltpu.VMEM((ALL_HEADS + 8, E), F32), pltpu.VMEM((16, E), F32), pltpu.VMEM((GROUP, 8, E), F32),
             pltpu.VMEM((stages + 1, GROUP, 8, E), F32), pltpu.VMEM((stages, GROUP, 8, E), F32),
             dma(()), dma(()), dma(()), dma((2, 6)), dma((2, 6)), dma((2, 3)), dma((2, 3)), dma((2, 3)), dma((2, 3)),
             dma((2, 6)), dma((6,)), dma((GROUP,)), dma((stages + 1,)), dma((stages + 1,)), dma((GROUP,)),

time: 134 us -> 134 us (level)
  no operation moved by 1% of the time
where the time goes in v5:
time: 134 us
  Pallas kernels  132 us (99%)
  local copies, waits for them, and re-layouts  1.37 us (1%)
    pallas_call x1, Pallas kernels, per_device(): pl.pallas_call(functools.partial(kernel, x_count, z_count), name='attenti...  129 us
    pallas_call x1, Pallas kernels, per_device(): pl.pallas_call(finish_kernel, name='finish', out_shape=outs, in_specs=[vm...  2.73 us

profile of v5, /device:TPU:1, one launch (start us, length us, event | category | flops | bytes accessed | tf_op | source)
XLA Modules:
  0.0 133.8 jit_solution(6244498352500159327)
XLA Ops:
  0.6 0.0 copy-start.1
  0.6 0.6 copy-done.1
  1.3 0.0 copy-start
  1.3 0.7 copy-done
  2.0 129.1 %attention.1 = (bf16[1,128,4096]{2,1,0:T(8,128)(2,1)S(1)}, bf16[1,128,4096]{2,1,0:T(8,128)(2,1)S(1)}, bf16[1,128,4096]{2,1,0:T(8,128)(2,1)S(1)}, bf16[1,128,4096...) custom-call(bf16[1,128,4096]{2,1,0:T(8,128)(2,1)} %q_ref.1, ...), custom_call_target="tpu_custom_call" | custom-call | tf_op jit(solution)/shard_map/attention/pallas_call | solution.py:517
  131.1 2.7 %finish.1 = (bf16[1,128,4096]{2,1,0:T(8,128)(2,1)}, bf16[1,128,4096]{2,1,0:T(8,128)(2,1)}, bf16[1,128,4096]{2,1,0:T(8,128)(2,1)}, bf16[1,128,4096]{2,1,0:T(8,128...) custom-call(bf16[1,128,4096]{2,1,0:T(8,128)(2,1)S(1)} %get-tuple-element.21.refs_0_, ...), custom_call_target="tpu_custom_call" | custom-call | tf_op jit(solution)/shard_map/finish/pallas_call | solution.py:536
Async XLA Ops:
  0.6 0.7 copy-start.1
  1.3 0.7 copy-start
